TPU v7x, 32 devices: a whole 2x2x4 slice. The times are simulated.
32 devices in a mesh: row: 4 (over z), col: 8 (over y, x, core).
Axes of the slice: x: 2, y: 2, z: 4, core: 2. Of those that a mesh axis runs over, the one named last changes fastest.
Arguments:
- features: bfloat16 [131072, 128], P(('row', 'col')), may hold values from -6 to 6
- neighbors: int32 [131072, 10], P(('row', 'col')), may hold values from 0 to 7167, as said below
- counts: int32 [131072], P(('row', 'col')), may hold values from 1 to 10
- hub_rows: int32 [4096], P(('row', 'col')), may hold values from 0 to 4095, as said below
- w_self: bfloat16 [128, 256], replicated, may hold values from -0.5 to 0.5
- w_neigh: bfloat16 [128, 256], replicated, may hold values from -0.5 to 0.5
- out_bias: float32 [256], replicated, may hold values from -3 to 3
- cotangent: bfloat16 [131072, 256], P(('row', 'col')), may hold values from -6 to 6
Outputs:
- activations: bfloat16 [131072, 256], P(('row', 'col'))
- grad_features: bfloat16 [131072, 128], P(('row', 'col'))
- grad_w_self: float32 [128, 256], replicated
- grad_w_neigh: float32 [128, 256], replicated
- grad_bias: float32 [256], replicated
Inputs may be any that keep to these rules, and one draw needn't show every extreme that they name: `neighbors`: rows below 1024 are never used by a partition of row 0, rows 5120 to 6143 never by one of the last row; slots at or past a node's count hold valid rows and are ignored. `hub_rows`: the 128 rows of one partition are distinct.
All inputs are finite; a program needn't handle non-finite values.
Results may differ from a plain program's by a relative error of at most 0.0075.
Values may be sent and summed in bfloat16 or wider, within the bound.
A program may use at most 256 MiB of HBM per device.

v0:
```python
import jax
import jax.numpy as jnp
from jax import lax
from jax.sharding import PartitionSpec as P

FANOUT = 10
HALO = 1024


def padded_2(cells, sides, width):
    for axis, dim in sides:
        count = lax.axis_size(axis)
        ends = count - 1
        head = lax.slice_in_dim(cells, 0, width, axis=dim)
        tail = lax.slice_in_dim(cells, cells.shape[dim] - width, cells.shape[dim], axis=dim)
        cells = jnp.concatenate(
            [
                lax.ppermute(tail, axis, [(i, (i + 1) % count) for i in range(ends)]),
                cells,
                lax.ppermute(head, axis, [((i + 1) % count, i) for i in range(ends)]),
            ],
            axis=dim,
        )
    return cells


def gelu_tanh(value):
    return jax.nn.gelu(value, approximate=True)


def on_device(features, neighbors, counts, hub_rows, w_self, w_neigh, out_bias, cotangent):
    node_count = features.shape[0]
    padded = padded_2(features, (("row", 0),), HALO)
    hub_local = jnp.take(features, hub_rows, axis=0)
    hub_table = lax.all_gather(hub_local, "col", axis=0, tiled=True)
    table = jnp.concatenate([padded, hub_table], axis=0)
    extent = table.shape[0]
    active = jnp.arange(FANOUT)[None, :] < counts[:, None]
    divisor = counts.astype(jnp.float32)[:, None]
    picked = jnp.take(table, neighbors, axis=0).astype(jnp.float32)
    agg = (jnp.sum(jnp.where(active[:, :, None], picked, 0.0), axis=1) / divisor).astype(
        jnp.bfloat16
    )
    pre = (
        jnp.dot(features, w_self, preferred_element_type=jnp.float32)
        + jnp.dot(agg, w_neigh, preferred_element_type=jnp.float32)
        + out_bias
    )
    act, backward = jax.vjp(gelu_tanh, pre)
    activations = act.astype(jnp.bfloat16)
    dz = backward(cotangent.astype(jnp.float32))[0].astype(jnp.bfloat16)
    dims = (((0,), (0,)), ((), ()))
    back_dims = (((1,), (1,)), ((), ()))
    grad_self = lax.dot_general(features, dz, dims, preferred_element_type=jnp.float32)
    grad_b = jnp.sum(dz.astype(jnp.float32), axis=0)
    grad_neigh = lax.dot_general(agg, dz, dims, preferred_element_type=jnp.float32)
    source = lax.dot_general(dz, w_neigh, back_dims, preferred_element_type=jnp.float32) / divisor
    grad_width = source.shape[1]
    values = jnp.where(active[:, :, None], source[:, None, :], 0.0)
    d_table = (
        jnp.zeros((extent, grad_width), jnp.float32)
        .at[neighbors.reshape(-1)]
        .add(values.reshape(-1, grad_width))
    )
    border_grads = jnp.concatenate(
        [d_table[:HALO], d_table[HALO + node_count : 2 * HALO + node_count]], axis=0
    )
    returned = padded_2(border_grads.astype(jnp.bfloat16), (("row", 0),), HALO).astype(
        border_grads.dtype
    )
    from_above = returned[:HALO]
    from_below = returned[returned.shape[0] - HALO :]
    mine = d_table[HALO : HALO + node_count]
    mine = mine.at[:HALO].add(from_above)
    mine = mine.at[node_count - HALO :].add(from_below)
    hub_share = lax.psum_scatter(
        d_table[2 * HALO + node_count :].astype(jnp.bfloat16),
        "col",
        scatter_dimension=0,
        tiled=True,
    ).astype(jnp.float32)
    mine = mine.at[hub_rows].add(hub_share)
    local_grad = lax.dot_general(dz, w_self, back_dims, preferred_element_type=jnp.float32)
    grad_features = (local_grad + mine).astype(jnp.bfloat16)
    grad_self, grad_neigh, grad_b = lax.psum((grad_self, grad_neigh, grad_b), ("row", "col"))
    return (activations, grad_features, grad_self, grad_neigh, grad_b)


def solution(mesh):
    placed = (
        P(("row", "col"), None),
        P(("row", "col"), None),
        P(("row", "col")),
        P(("row", "col")),
        P(),
        P(),
        P(),
        P(("row", "col"), None),
    )
    return jax.shard_map(
        on_device,
        mesh=mesh,
        in_specs=placed,
        out_specs=(P(("row", "col"), None), P(("row", "col"), None), P(), P(), P()),
        check_vma=False,
    )
```

profile of v0, /device:TPU:0, one launch (start us, length us, event | category | flops | bytes accessed | tf_op | source)
XLA Modules:
  0.0 690.5 jit_solution(11645842956365100980)
XLA Ops:
  8.1 2.0 fusion.22
  10.0 5.6 collective-permute-start
  19.3 1.7 compare_select_fusion.1
  21.7 2.5 iota_compare_fusion
  24.2 3.1 copy.17
  28.1 9.3 %all_gather.3 = bf16[1024,128]{1,0:T(8,128)(2,1)S(1)} all-gather(bf16[128,128]{1,0:T(8,128)(2,1)S(1)} %broadcast_select_fusion), channel_id=1, replica_groups=mesh['row'=4,'col'=8] {'col'}, dimensions={0}, use_global_device_ids=true | all-gather | bytes 294912 | tf_op jit(solution)/shard_map/all_gather | solution.py:35
  38.9 2.7 lt.61
  43.2 2.4 reshape.142
  46.5 3.4 reshape.131
  50.8 2.7 fusion.23
  54.7 143.6 %gather_fusion.1 = bf16[40960,128]{1,0:T(8,128)(2,1)} fusion(bf16[7168,128]{1,0:T(8,128)(2,1)S(1)} %pad_maximum_fusion, s32[40960]{0:T(1024)S(1)} %broadcast_clamp_fusion), kind=kCustom, calls=%fused_computation.1 | custom fusion | bytes 21135360 | tf_op jit(solution)/shard_map/jit(_take)/gather | solution.py:40
  198.2 19.5 %reshape.141 = bf16[4096,10,128]{2,1,0:T(8,128)(2,1)} reshape(bf16[40960,128]{1,0:T(8,128)(2,1)} %gather_fusion.1) | data formatting | bytes 20971520 | tf_op jit(solution)/shard_map/jit(_take)/gather | solution.py:40
  217.7 24.5 %select_reduce_fusion = f32[4096,128]{1,0:T(8,128)S(1)} fusion(bf16[4096,10,128]{2,1,0:T(8,128)(2,1)} %reshape.141, pred[4096,10]{1,0:T(8,128)(4,1)S(1)} %copy-done.8, pred[4096,10]{1,0:T(8,128)(4,1)S(1)} %copy-done.7), kind=kLoop, calls=%fused_computation.4 | loop fusion | flops 20447232 | bytes 12664832 | tf_op jit(solution)/shard_map/reduce_sum | solution.py:41
  243.0 5.5 convert_reduce_fusion
  250.8 11.0 %broadcast_in_dim.80 = f32[4096,10,128]{2,1,0:T(8,128)} broadcast(f32[4096,128]{1,0:T(8,128)S(1)} %convolution_divide_fusion), dimensions={0,2} | broadcast | bytes 23068672 | tf_op jit(solution)/shard_map/jit(_where)/broadcast_in_dim | solution.py:59
  261.9 27.5 %broadcast_in_dim.81 = f32[40960,128]{1,0:T(8,128)} reshape(f32[4096,10,128]{2,1,0:T(8,128)} %broadcast_in_dim.80) | data formatting | bytes 41943040 | tf_op jit(solution)/shard_map/jit(_where)/broadcast_in_dim | solution.py:59
  289.4 243.6 %scatter_custom_fusion = f32[7168,128]{1,0:T(8,128)} fusion(s32[40960]{0:T(1024)} %bitcast.15, f32[40960,128]{1,0:T(8,128)} %broadcast_in_dim.81, f32[]{:T(128)} %constant.96.clone.1, pred[40960]{0:T(1024)(128)(4,1)S(1)} %copy-done.10), kind=kCustom, calls=%fused_computation.5 | custom fusion | flops 10485760 | bytes 24683520 | tf_op jit(solution)/shard_map/scatter-add | solution.py:63
  533.0 2.4 convert.7
  537.5 6.0 collective-permute-start.2
  545.6 39.4 %psum.23 = f32[256]{0:T(256)} all-reduce(f32[256]{0:T(256)S(1)} %copy-done.12), channel_id=1, replica_groups=mesh['row'=4,'col'=8] {'row','col'}, use_global_device_ids=true, to_apply=%region_7.8 | all-reduce | flops 256 | bytes 2048 | tf_op jit(solution)/shard_map/psum | solution.py:85
  585.0 84.3 %all-reduce.3.cloned.1.call-done = (f32[128,256]{0,1:T(8,128)}, f32[128,256]{1,0:T(8,128)}) async-done(((f32[128,256]{0,1:T(8,128)}, f32[128,256]{1,0:T(8,128)}), (f32[128,256]{0,1:T(8,128)}, f32[128,256]{1,0:T(8,128)})) %all-reduce.3.cloned.1.call-update) | async-done | bytes 262160 | tf_op jit(solution)/shard_map/psum | solution.py:85
  673.4 2.0 convolution_add_fusion.1
  675.4 4.3 scatter_custom_fusion.1
  679.8 2.7 convert_element_type.40
  (66 shorter events, 23.1 us)
Async XLA Ops:
  8.0 235.0 %copy-start = (bf16[128,256]{1,0:T(8,128)(2,1)S(1)}, bf16[128,256]{1,0:T(8,128)(2,1)}, u32[]{:S(2)}) copy-start(bf16[128,256]{1,0:T(8,128)(2,1)} %param.17) | copy-start | bytes 196612
  8.0 19.3 %copy-start.1 = (bf16[4096,128]{1,0:T(8,128)(2,1)S(1)}, bf16[4096,128]{1,0:T(8,128)(2,1)}, u32[]{:S(2)}) copy-start(bf16[4096,128]{1,0:T(8,128)(2,1)} %param.12) | copy-start | bytes 3145732
  8.0 661.3 %all-reduce.3.cloned.1.call-start = ((), (), s32[]{:S(2)}) async-start(), calls=%async_computation.2 | async-start | bytes 524288 | tf_op jit(solution)/shard_map/psum | solution.py:85
  10.0 43.5 %collective-permute-start = (bf16[1024,128]{1,0:T(8,128)(2,1)}, bf16[1024,128]{1,0:T(8,128)(2,1)}, u32[]{:S(2)}, u32[]{:S(2)}) collective-permute-start(bf16[1024,128]{1,0:T(8,128)(2,1)} %get-tuple-element.47), channel_id=1, source_target_pairs={{0,8},{8,16},{16,24},{1,9},{9,17},{17,25},{2,10},{10,18},{18,26},{... | collective-permute-start | bytes 786440 | tf_op jit(solution)/shard_map/ppermute | solution.py:18
  15.7 37.8 %collective-permute-start.1 = (bf16[1024,128]{1,0:T(8,128)(2,1)}, bf16[1024,128]{1,0:T(8,128)(2,1)}, u32[]{:S(2)}, u32[]{:S(2)}) collective-permute-start(bf16[1024,128]{1,0:T(8,128)(2,1)} %get-tuple-element.48), channel_id=1, source_target_pairs={{8,0},{16,8},{24,16},{9,1},{17,9},{25,17},{10,2},{18,10},{26,18},{... | collective-permute-start | bytes 786440 | tf_op jit(solution)/shard_map/ppermute | solution.py:20
  17.6 10.4 %copy-start.13 = (s32[128]{0:T(128)}, s32[128]{0:T(128)S(1)}, u32[]{:S(2)}) copy-start(s32[128]{0:T(128)S(1)} %compare_select_fusion.2) | copy-start | bytes 1540
  24.2 14.7 %copy-start.6 = (pred[4096,10]{1,0:T(8,128)(4,1)}, pred[4096,10]{1,0:T(8,128)(4,1)S(1)}, u32[]{:S(2)}) copy-start(pred[4096,10]{1,0:T(8,128)(4,1)S(1)} %iota_compare_fusion) | copy-start | bytes 122884
  41.6 9.2 %copy-start.9 = (bf16[128,256]{1,0:T(8,128)(2,1)S(1)}, bf16[128,256]{1,0:T(8,128)(2,1)}, u32[]{:S(2)}) copy-start(bf16[128,256]{1,0:T(8,128)(2,1)} %param.16) | copy-start | bytes 196612
  198.2 19.5 %copy-start.7 = (pred[4096,10]{1,0:T(8,128)(4,1)S(1)}, pred[4096,10]{1,0:T(8,128)(4,1)}, u32[]{:S(2)}) copy-start(pred[4096,10]{1,0:T(8,128)(4,1)} %copy-done.6) | copy-start | bytes 122884
  198.2 19.5 %copy-start.8 = (pred[4096,10]{1,0:T(8,128)(4,1)S(1)}, pred[4096,10]{1,0:T(8,128)(4,1)}, u32[]{:S(2)}) copy-start(pred[4096,10]{1,0:T(8,128)(4,1)} %copy.15) | copy-start | bytes 122884
  217.7 25.3 %copy-start.5 = (f32[4096,256]{1,0:T(8,128)S(1)}, f32[4096,256]{1,0:T(8,128)}, u32[]{:S(2)}) copy-start(f32[4096,256]{1,0:T(8,128)} %fusion.23) | copy-start | bytes 12582916
  217.7 25.3 %copy-start.14 = (bf16[4096,256]{1,0:T(8,128)(2,1)S(1)}, bf16[4096,256]{1,0:T(8,128)(2,1)}, u32[]{:S(2)}) copy-start(bf16[4096,256]{1,0:T(8,128)(2,1)} %param.19) | copy-start | bytes 6291460
  217.7 25.3 %copy-start.15 = (f32[256]{0:T(256)S(1)}, f32[256]{0:T(256)}, u32[]{:S(2)}) copy-start(f32[256]{0:T(256)} %param.18) | copy-start | bytes 3076
  248.6 2.3 copy-start.2
  261.9 27.5 %copy-start.10 = (pred[40960]{0:T(1024)(128)(4,1)S(1)}, pred[40960]{0:T(1024)(128)(4,1)}, u32[]{:S(2)}) copy-start(pred[40960]{0:T(1024)(128)(4,1)} %lt.61) | copy-start | bytes 122884
  533.0 10.6 %copy-start.3 = (bf16[4096,256]{1,0:T(8,128)(2,1)S(1)}, bf16[4096,256]{1,0:T(8,128)(2,1)}, u32[]{:S(2)}) copy-start(bf16[4096,256]{1,0:T(8,128)(2,1)} %copy-done.2) | copy-start | bytes 6291460
  536.2 134.8 %collective-permute-start.3 = (bf16[1024,128]{1,0:T(8,128)(2,1)S(1)}, bf16[1024,128]{1,0:T(8,128)(2,1)}, u32[]{:S(2)}, u32[]{:S(2)}) collective-permute-start(bf16[1024,128]{1,0:T(8,128)(2,1)S(1)} %get-tuple-element.45), channel_id=1, source_target_pairs={{8,0},{16,8},{24,16},{9,1},{17,9},{25,17},{10,2},{18,10},{26,18},{... | collective-permute-start | bytes 786440 | tf_op jit(solution)/shard_map/ppermute | solution.py:20
  537.5 8.1 %copy-start.12 = (f32[256]{0:T(256)S(1)}, f32[256]{0:T(256)}, u32[]{:S(2)}) copy-start(f32[256]{0:T(256)} %get-tuple-element.41) | copy-start | bytes 3076
  537.5 133.5 %slice-start = ((f32[7168,128]{1,0:T(8,128)}), f32[4096,128]{1,0:T(8,128)S(1)}, s32[]{:S(2)}) async-start(f32[7168,128]{1,0:T(8,128)} %scatter_custom_fusion), calls=%async_computation.3 | async-start | bytes 4194304 | tf_op jit(solution)/shard_map/slice | solution.py:73
  537.5 133.5 %collective-permute-start.2 = (bf16[1024,128]{1,0:T(8,128)(2,1)}, bf16[1024,128]{1,0:T(8,128)(2,1)}, u32[]{:S(2)}, u32[]{:S(2)}) collective-permute-start(bf16[1024,128]{1,0:T(8,128)(2,1)} %get-tuple-element.46), channel_id=1, source_target_pairs={{0,8},{8,16},{16,24},{1,9},{9,17},{17,25},{2,10},{10,18},{18,26},{... | collective-permute-start | bytes 786440 | tf_op jit(solution)/shard_map/ppermute | solution.py:18
  545.0 130.4 %reduce-scatter.2.cloned.1.call-start = ((), (), s32[]{:S(2)}) async-start(), calls=%async_computation.1 | async-start | bytes 294912 | tf_op jit(solution)/shard_map/reduce_scatter | solution.py:76
  671.0 2.4 copy-start.4
  675.4 7.0 %copy-start.11 = (f32[128,256]{1,0:T(8,128)S(1)}, f32[128,256]{1,0:T(8,128)}, u32[]{:S(2)}) copy-start(f32[128,256]{1,0:T(8,128)} %get-tuple-element.52) | copy-start | bytes 393220
Sparse Core Ops, SparseCore 0:
  545.1 124.1 all-reduce.2
Sparse Core Ops, SparseCore 1:
  549.1 32.6 reduce-scatter.1
where the time goes:
time: 693 us; the launch traced here: 691 us
  other arithmetic  291 us (42%)
  local copies, waits for them, and re-layouts  222 us (32%)
  waiting for transfers between devices  84.9 us (12%)
  blocking collectives  48.7 us (7%)
  between operations  15.7 us (2%)
  starting transfers between devices  14.3 us (2%)
  matrix products  14 us (2%)
    scatter-add x1, other arithmetic, on_device(): d_table = jnp.zeros((extent, grad_width), jnp.float32).at[neighbors.resha...  244 us
    gather x2, local copies, waits for them, and re-layouts, on_device(): picked = jnp.take(table, neighbors, axis=0).astype(jnp.float32)  163 us
    psum x1, waiting for transfers between devices, on_device(): lax.psum((grad_self, grad_neigh, grad_b), ('row', 'col'))  84.3 us
    psum x1, blocking collectives, on_device(): lax.psum((grad_self, grad_neigh, grad_b), ('row', 'col'))  39.4 us
    broadcast_in_dim x2, local copies, waits for them, and re-layouts, on_device(): values = jnp.where(active[:, :, None], source[:, None, :], 0.0)  38.6 us
    reduce_sum x1, other arithmetic, on_device(): jnp.sum(jnp.where(active[:, :, None], picked, 0.0), axis=1) / divisor  24.5 us
  transfers between devices with their start and end apart: 6, of which 1 were waited for; matrix products, arithmetic and copies ran while one was open for 5% of the time, Pallas kernels for 0%

commit v1 on v0

v1 whole, which is shorter than its diff:
```python
import functools

import jax
import jax.numpy as jnp
from jax import lax
from jax.experimental import pallas as pl
from jax.experimental.pallas import tpu as pltpu
from jax.sharding import PartitionSpec as P

FANOUT = 10
HALO = 1024
UNROLL = 8
PAD = 8
VMEM_LIMIT = 60 * 1024 * 1024


def gather_kernel(rows_ref, lower_ref, own_ref, upper_ref, hub_ref, total_ref, table):
    at = 0
    for part in (lower_ref, own_ref, upper_ref, hub_ref):
        size = part.shape[0]
        table[at : at + size, :] = part[...].astype(jnp.float32)
        at += size
    table[at : at + PAD, :] = jnp.zeros((PAD, table.shape[1]), jnp.float32)

    def step(i, carry):
        for u in range(UNROLL):
            n = i * UNROLL + u
            picked = [table[pl.ds(rows_ref[s, n], 1), :] for s in range(FANOUT)]
            while len(picked) > 1:
                picked = [a + b for a, b in zip(picked[::2], picked[1::2])] + (
                    [picked[-1]] if len(picked) % 2 else []
                )
            total_ref[pl.ds(n, 1), :] = picked[0]
        return carry

    lax.fori_loop(0, total_ref.shape[0] // UNROLL, step, 0)


def gather_sum(rows, lower, own, upper, hubs):
    extent = lower.shape[0] + own.shape[0] + upper.shape[0] + hubs.shape[0]
    vmem = pl.BlockSpec(memory_space=pltpu.VMEM)
    return pl.pallas_call(
        gather_kernel,
        out_shape=jax.ShapeDtypeStruct(own.shape, jnp.float32),
        in_specs=[pl.BlockSpec(memory_space=pltpu.SMEM)] + [vmem] * 4,
        out_specs=vmem,
        scratch_shapes=[pltpu.VMEM((extent + PAD, own.shape[1]), jnp.float32)],
        compiler_params=pltpu.CompilerParams(vmem_limit_bytes=VMEM_LIMIT),
        name="gather_sum",
    )(rows, lower, own, upper, hubs)


def scatter_kernel(rows_ref, source_ref, own_ref, border_ref, hub_ref, *sums):
    chunk = 512
    extent = sums[0].shape[0]
    width = sums[0].shape[1]
    kinds = len(sums)

    def clear(i, carry):
        for total in sums:
            total[pl.ds(pl.multiple_of(i * chunk, chunk), chunk), :] = jnp.zeros(
                (chunk, width), jnp.float32
            )
        return carry

    lax.fori_loop(0, extent // chunk, clear, 0)

    def step(i, carry):
        for u in range(UNROLL):
            n = i * UNROLL + u
            value = source_ref[pl.ds(n, 1), :]
            for first in range(0, FANOUT, kinds):
                rows = [rows_ref[first + k, n] for k in range(kinds)]
                held = [sums[k][pl.ds(rows[k], 1), :] for k in range(kinds)]
                for k in range(kinds):
                    sums[k][pl.ds(rows[k], 1), :] = held[k] + value
        return carry

    lax.fori_loop(0, source_ref.shape[0] // UNROLL, step, 0)

    def added(at, size):
        total = sums[0][pl.ds(at, size), :]
        for other in sums[1:]:
            total = total + other[pl.ds(at, size), :]
        return total

    def emit(ref, ref_at, at, count):
        def one(i, carry):
            off = pl.multiple_of(i * 128, 128)
            ref[pl.ds(ref_at + off, 128), :] = added(at + off, 128).astype(ref.dtype)
            return carry

        lax.fori_loop(0, count // 128, one, 0)

    nodes = own_ref.shape[0]
    emit(border_ref, 0, 0, HALO)
    emit(own_ref, 0, HALO, nodes)
    emit(border_ref, HALO, HALO + nodes, HALO)
    emit(hub_ref, 0, 2 * HALO + nodes, hub_ref.shape[0])


def scatter_sum(rows, source, hubs):
    nodes, width = source.shape
    extent = 2 * HALO + nodes + hubs
    kinds = 10 if extent <= 8192 else 5
    vmem = pl.BlockSpec(memory_space=pltpu.VMEM)
    return pl.pallas_call(
        scatter_kernel,
        out_shape=(
            jax.ShapeDtypeStruct((nodes, width), jnp.float32),
            jax.ShapeDtypeStruct((2 * HALO, width), jnp.bfloat16),
            jax.ShapeDtypeStruct((hubs, width), jnp.bfloat16),
        ),
        in_specs=[pl.BlockSpec(memory_space=pltpu.SMEM), vmem],
        out_specs=(vmem, vmem, vmem),
        scratch_shapes=[pltpu.VMEM((extent + PAD, width), jnp.float32)] * kinds,
        compiler_params=pltpu.CompilerParams(vmem_limit_bytes=VMEM_LIMIT),
        name="scatter_sum",
    )(rows, source)


def rims(head, tail, axis):
    count = lax.axis_size(axis)
    ends = count - 1
    return (
        lax.ppermute(tail, axis, [(i, i + 1) for i in range(ends)]),
        lax.ppermute(head, axis, [(i + 1, i) for i in range(ends)]),
    )


def gelu_tanh(value):
    return jax.nn.gelu(value, approximate=True)


def on_device(features, neighbors, counts, hub_rows, w_self, w_neigh, out_bias, cotangent):
    node_count = features.shape[0]
    lower, upper = rims(features[:HALO], features[node_count - HALO :], "row")
    hub_local = jnp.take(features, hub_rows, axis=0)
    hub_table = lax.all_gather(hub_local, "col", axis=0, tiled=True)
    hubs = hub_table.shape[0]
    extent = 2 * HALO + node_count + hubs
    active = jnp.arange(FANOUT)[:, None] < counts[None, :]
    rows = jnp.where(active, neighbors.T, extent)
    divisor = counts.astype(jnp.float32)[:, None]
    agg = (gather_sum(rows, lower, features, upper, hub_table) / divisor).astype(jnp.bfloat16)
    pre = (
        jnp.dot(features, w_self, preferred_element_type=jnp.float32)
        + jnp.dot(agg, w_neigh, preferred_element_type=jnp.float32)
        + out_bias
    )
    act, backward = jax.vjp(gelu_tanh, pre)
    activations = act.astype(jnp.bfloat16)
    dz = backward(cotangent.astype(jnp.float32))[0].astype(jnp.bfloat16)
    dims = (((0,), (0,)), ((), ()))
    back_dims = (((1,), (1,)), ((), ()))
    grad_self = lax.dot_general(features, dz, dims, preferred_element_type=jnp.float32)
    grad_b = jnp.sum(dz.astype(jnp.float32), axis=0)
    grad_neigh = lax.dot_general(agg, dz, dims, preferred_element_type=jnp.float32)
    source = lax.dot_general(dz, w_neigh, back_dims, preferred_element_type=jnp.float32) / divisor
    mine, border, hub_grads = scatter_sum(rows, source, hubs)
    from_above, from_below = rims(border[:HALO], border[HALO:], "row")
    mine = mine.at[:HALO].add(from_above.astype(jnp.float32))
    mine = mine.at[node_count - HALO :].add(from_below.astype(jnp.float32))
    hub_share = lax.psum_scatter(hub_grads, "col", scatter_dimension=0, tiled=True).astype(
        jnp.float32
    )
    mine = mine.at[hub_rows].add(hub_share)
    local_grad = lax.dot_general(dz, w_self, back_dims, preferred_element_type=jnp.float32)
    grad_features = (local_grad + mine).astype(jnp.bfloat16)
    grad_self, grad_neigh, grad_b = lax.psum((grad_self, grad_neigh, grad_b), ("row", "col"))
    return (activations, grad_features, grad_self, grad_neigh, grad_b)


def solution(mesh):
    placed = (
        P(("row", "col"), None),
        P(("row", "col"), None),
        P(("row", "col")),
        P(("row", "col")),
        P(),
        P(),
        P(),
        P(("row", "col"), None),
    )
    return jax.shard_map(
        on_device,
        mesh=mesh,
        in_specs=placed,
        out_specs=(P(("row", "col"), None), P(("row", "col"), None), P(), P(), P()),
        check_vma=False,
    )
```

time: 693 us -> 318 us (0.46)
  other arithmetic: 291 us -> 16.7 us
  local copies, waits for them, and re-layouts: 222 us -> 8.09 us
  Pallas kernels: 0 us -> 115 us
    scatter-add x3 -> x2, other arithmetic: 246 us -> 3.76 us  [the longest x1 1.88 us: on_device(): mine = mine.at[node_count - HALO:].add(from_below.astype(jnp.float32))]
    gather x2 -> x0, local copies, waits for them, and re-layouts: 163 us -> none  [on_device(): picked = jnp.take(table, neighbors, axis=0).astype(jnp.float32)]
    pallas_call x0 -> x2, Pallas kernels: none -> 115 us  [the longest x1 59.3 us: scatter_sum(): pl.pallas_call(scatter_kernel, out_shape=(jax.ShapeDtypeStruct((nodes, wi...]
    broadcast_in_dim x3 -> x0, local copies, waits for them, and re-layouts: 40.9 us -> none  [the longest x2 38.6 us: on_device(): values = jnp.where(active[:, :, None], source[:, None, :], 0.0)]
    reduce_sum x1 -> x0, other arithmetic: 24.5 us -> none  [on_device(): jnp.sum(jnp.where(active[:, :, None], picked, 0.0), axis=1) / divisor]
  transfers between devices with their start and end apart: 6 -> 6, of which waited for: 1 -> 1; matrix products, arithmetic and copies ran while one was open for 5% -> 6% of each run, Pallas kernels for 0% -> 0%
where the time goes in v1:
time: 318 us; the launch traced here: 317 us
  Pallas kernels  115 us (36%)
  waiting for transfers between devices  81.5 us (26%)
  blocking collectives  51.5 us (16%)
  matrix products  17.3 us (5%)
  other arithmetic  16.7 us (5%)
  between operations  15.6 us (5%)
  starting transfers between devices  11.7 us (4%)
  local copies, waits for them, and re-layouts  8.09 us (3%)
    psum x1, waiting for transfers between devices, on_device(): lax.psum((grad_self, grad_neigh, grad_b), ('row', 'col'))  81.4 us
    pallas_call x1, Pallas kernels, scatter_sum(): pl.pallas_call(scatter_kernel, out_shape=(jax.ShapeDtypeStruct((nodes, wi...  59.3 us
    pallas_call x1, Pallas kernels, gather_sum(): pl.pallas_call(gather_kernel, out_shape=jax.ShapeDtypeStruct(own.shape, j...  55.2 us
    psum x1, blocking collectives, on_device(): lax.psum((grad_self, grad_neigh, grad_b), ('row', 'col'))  40.8 us
    all_gather x1, blocking collectives, on_device(): hub_table = lax.all_gather(hub_local, 'col', axis=0, tiled=True)  10.8 us
    ppermute x2, starting transfers between devices, rims(): lax.ppermute(tail, axis, [(i, i + 1) for i in range(ends)])  9.05 us
    dot_general x1, matrix products, on_device(): jnp.dot(agg, w_neigh, preferred_element_type=jnp.float32)  6.57 us
  transfers between devices with their start and end apart: 6, of which 1 were waited for; matrix products, arithmetic and copies ran while one was open for 6% of the time, Pallas kernels for 0%

profile of v1, /device:TPU:0, one launch (start us, length us, event | category | flops | bytes accessed | tf_op | source)
XLA Modules:
  0.0 316.9 jit_solution(520776165735203225)
XLA Ops:
  8.1 1.2 fusion.15
  9.2 1.3 collective-permute-start.1
  10.5 5.6 %collective-permute-start = (bf16[1024,128]{1,0:T(8,128)(2,1)S(1)}, bf16[1024,128]{1,0:T(8,128)(2,1)S(1)}, u32[]{:S(2)}, u32[]{:S(2)}) collective-permute-start(bf16[1024,128]{1,0:T(8,128)(2,1)S(1)} %get-tuple-element.46), channel_id=1, source_target_pairs={{0,8},{8,16},{16,24},{1,9},{9,17},{17,25},{2,10},{10,18},{18,26},{... | collective-permute-start | bytes 786440 | tf_op jit(solution)/shard_map/ppermute | solution.py:126
  18.2 2.0 gather_fusion
  20.3 10.8 %all_gather.3.hub_ref = bf16[1024,128]{1,0:T(8,128)(2,1)} all-gather(bf16[128,128]{1,0:T(8,128)(2,1)S(1)} %broadcast_select_fusion), channel_id=1, replica_groups=mesh['row'=4,'col'=8] {'col'}, dimensions={0}, use_global_device_ids=true | all-gather | bytes 294912 | tf_op jit(solution)/shard_map/all_gather | solution.py:139
  31.1 1.7 bitcast_select_fusion.rows_ref
  32.8 2.6 fusion.17
  36.8 55.2 %gather_sum.1 = f32[4096,128]{1,0:T(8,128)} custom-call(s32[10,4096]{1,0:T(8,128)} %bitcast_select_fusion.rows_ref, bf16[1024,128]{1,0:T(8,128)(2,1)} %copy-done.5, bf16[4096,128]{1,0:T(8,128)(2,1)} %own_ref.1, bf16[1024,128]{1,0:T(8,128)(2,1)} %copy-done.4, bf16[1024,128]{1,0:T(8,128)(2,1)} %all_gather.3.hub_ref), custom_call_target="tpu_custom_call" | custom-call | tf_op jit(solution)/shard_map/gather_sum/pallas_call | solution.py:42
  92.0 2.1 divide_convert_fusion
  94.2 6.6 %convert_reduce_fusion = (f32[256]{0:T(256)S(1)}, bf16[4096,256]{1,0:T(8,128)(2,1)S(1)}, bf16[4096,256]{1,0:T(8,128)(2,1)}) fusion(bf16[4096,256]{1,0:T(8,128)(2,1)S(1)} %copy-done.7, f32[256]{0:T(256)S(1)} %copy-done.8, f32[4096,256]{1,0:T(8,128)} %fusion.17, bf16[4096,128]{1,0:T(8,128)(2,1)S(1)} %divide_convert_fusion, bf16[128,256]{1,0:T(8,128)(2,1)S(1)} %copy-done), kind=kOutput, calls=%fused_computation.20 | convolution fusion | flops 296746752 | bytes 11601920 | tf_op jit(solution)/shard_map/dot_general | solution.py:148
  100.8 1.2 fusion.18
  102.0 1.9 convolution_divide_fusion.source_ref
  103.8 59.3 %scatter_sum.1 = (f32[4096,128]{1,0:T(8,128)}, bf16[2048,128]{1,0:T(8,128)(2,1)}, bf16[1024,128]{1,0:T(8,128)(2,1)}) custom-call(s32[10,4096]{1,0:T(8,128)} %bitcast_select_fusion.rows_ref, f32[4096,128]{1,0:T(8,128)} %convolution_divide_fusion.source_ref), custom_call_target="tpu_custom_call" | custom-call | tf_op jit(solution)/shard_map/scatter_sum/pallas_call | solution.py:107
  164.3 3.5 %collective-permute-start.2 = (bf16[1024,128]{1,0:T(8,128)(2,1)S(1)}, bf16[1024,128]{1,0:T(8,128)(2,1)S(1)}, u32[]{:S(2)}, u32[]{:S(2)}) collective-permute-start(bf16[1024,128]{1,0:T(8,128)(2,1)S(1)} %get-tuple-element.48), channel_id=1, source_target_pairs={{0,8},{8,16},{16,24},{1,9},{9,17},{17,25},{2,10},{10,18},{18,26},{... | collective-permute-start | bytes 786440 | tf_op jit(solution)/shard_map/ppermute | solution.py:126
  167.8 1.4 convolution_bitcast_fusion
  169.2 1.3 collective-permute-start.3
  170.6 40.8 %psum.23 = f32[256]{0:T(256)} all-reduce(f32[256]{0:T(256)S(1)} %get-tuple-element.42), channel_id=1, replica_groups=mesh['row'=4,'col'=8] {'row','col'}, use_global_device_ids=true, to_apply=%region_5.6 | all-reduce | flops 256 | bytes 2048 | tf_op jit(solution)/shard_map/psum | solution.py:170
  211.3 81.4 %all-reduce.3.cloned.1.call-done = (f32[128,256]{0,1:T(8,128)}, f32[128,256]{1,0:T(8,128)}) async-done(((f32[128,256]{0,1:T(8,128)}, f32[128,256]{1,0:T(8,128)}), (f32[128,256]{0,1:T(8,128)}, f32[128,256]{1,0:T(8,128)})) %all-reduce.3.cloned.1.call-update) | async-done | bytes 262160 | tf_op jit(solution)/shard_map/psum | solution.py:170
  292.8 1.7 copy.13
  294.4 1.9 add_dynamic-update-slice_fusion
  296.3 1.9 fusion.11
  298.2 3.6 %convolution_add_fusion.1 = f32[4096,128]{1,0:T(8,128)} fusion(f32[4096,128]{1,0:T(8,128)} %fusion.11, bf16[4096,256]{1,0:T(8,128)(2,1)S(1)} %get-tuple-element.43, bf16[128,256]{1,0:T(8,128)(2,1)S(1)} %copy-done.3), kind=kOutput, calls=%fused_computation.8 | convolution fusion | flops 268959744 | bytes 6356992 | tf_op jit(solution)/shard_map/dot_general | solution.py:168
  301.8 4.3 %scatter_custom_fusion = f32[4096,128]{1,0:T(8,128)} fusion(f32[4096,128]{1,0:T(8,128)} %convolution_add_fusion.1, s32[128]{0:T(128)S(1)} %compare_select_fusion, bf16[128,128]{1,0:T(8,128)(2,1)} %reduce-scatter.2.cloned.1.call-done), kind=kCustom, calls=%fused_computation.29 | custom fusion | flops 32768 | bytes 2129920 | tf_op jit(solution)/shard_map/scatter-add | solution.py:167
  306.1 2.7 convert_element_type.38
  (34 shorter events, 5.5 us)
Async XLA Ops:
  8.0 86.1 %copy-start = (bf16[128,256]{1,0:T(8,128)(2,1)S(1)}, bf16[128,256]{1,0:T(8,128)(2,1)}, u32[]{:S(2)}) copy-start(bf16[128,256]{1,0:T(8,128)(2,1)} %param.17) | copy-start | bytes 196612
  8.0 24.7 %copy-start.1 = (bf16[4096,128]{1,0:T(8,128)(2,1)S(1)}, bf16[4096,128]{1,0:T(8,128)(2,1)}, u32[]{:S(2)}) copy-start(bf16[4096,128]{1,0:T(8,128)(2,1)} %own_ref.1) | copy-start | bytes 3145732
  8.0 24.7 %copy-start.3 = (bf16[128,256]{1,0:T(8,128)(2,1)S(1)}, bf16[128,256]{1,0:T(8,128)(2,1)}, u32[]{:S(2)}) copy-start(bf16[128,256]{1,0:T(8,128)(2,1)} %param.16) | copy-start | bytes 196612
  8.0 284.7 %all-reduce.3.cloned.1.call-start = ((), (), s32[]{:S(2)}) async-start(), calls=%async_computation.2 | async-start | bytes 524288 | tf_op jit(solution)/shard_map/psum | solution.py:170
  9.2 26.2 %collective-permute-start.1 = (bf16[1024,128]{1,0:T(8,128)(2,1)S(1)}, bf16[1024,128]{1,0:T(8,128)(2,1)S(1)}, u32[]{:S(2)}, u32[]{:S(2)}) collective-permute-start(bf16[1024,128]{1,0:T(8,128)(2,1)S(1)} %get-tuple-element.45), channel_id=1, source_target_pairs={{8,0},{16,8},{24,16},{9,1},{17,9},{25,17},{10,2},{18,10},{26,18},{... | collective-permute-start | bytes 786440 | tf_op jit(solution)/shard_map/ppermute | solution.py:127
  10.5 24.9 %collective-permute-start = (bf16[1024,128]{1,0:T(8,128)(2,1)S(1)}, bf16[1024,128]{1,0:T(8,128)(2,1)S(1)}, u32[]{:S(2)}, u32[]{:S(2)}) collective-permute-start(bf16[1024,128]{1,0:T(8,128)(2,1)S(1)} %get-tuple-element.46), channel_id=1, source_target_pairs={{0,8},{8,16},{16,24},{1,9},{9,17},{17,25},{2,10},{10,18},{18,26},{... | collective-permute-start | bytes 786440 | tf_op jit(solution)/shard_map/ppermute | solution.py:126
  35.4 0.7 copy-start.4
  36.1 0.7 copy-start.5
  92.0 2.2 copy-start.7
  92.0 2.2 copy-start.8
  103.8 63.9 %copy-start.2 = (bf16[4096,128]{1,0:T(8,128)(2,1)S(1)}, bf16[4096,128]{1,0:T(8,128)(2,1)}, u32[]{:S(2)}) copy-start(bf16[4096,128]{1,0:T(8,128)(2,1)} %own_ref.1) | copy-start | bytes 3145732
  164.3 130.2 %collective-permute-start.2 = (bf16[1024,128]{1,0:T(8,128)(2,1)S(1)}, bf16[1024,128]{1,0:T(8,128)(2,1)S(1)}, u32[]{:S(2)}, u32[]{:S(2)}) collective-permute-start(bf16[1024,128]{1,0:T(8,128)(2,1)S(1)} %get-tuple-element.48), channel_id=1, source_target_pairs={{0,8},{8,16},{16,24},{1,9},{9,17},{17,25},{2,10},{10,18},{18,26},{... | collective-permute-start | bytes 786440 | tf_op jit(solution)/shard_map/ppermute | solution.py:126
  169.2 132.6 %reduce-scatter.2.cloned.1.call-start = ((), (), s32[]{:S(2)}) async-start(), calls=%async_computation.1 | async-start | bytes 294912 | tf_op jit(solution)/shard_map/reduce_scatter | solution.py:164
  169.2 127.1 %collective-permute-start.3 = (bf16[1024,128]{1,0:T(8,128)(2,1)S(1)}, bf16[1024,128]{1,0:T(8,128)(2,1)S(1)}, u32[]{:S(2)}, u32[]{:S(2)}) collective-permute-start(bf16[1024,128]{1,0:T(8,128)(2,1)S(1)} %get-tuple-element.47), channel_id=1, source_target_pairs={{8,0},{16,8},{24,16},{9,1},{17,9},{25,17},{10,2},{18,10},{26,18},{... | collective-permute-start | bytes 786440 | tf_op jit(solution)/shard_map/ppermute | solution.py:127
  306.1 2.7 copy-start.6
Sparse Core Ops, SparseCore 0:
  169.3 123.4 all-reduce.2
Sparse Core Ops, SparseCore 1:
  172.7 31.9 reduce-scatter.1

commit v2 on v1

--- a/solution.py
+++ b/solution.py
@@ -119,13 +119,304 @@
     )(rows, source)
 
 
-def rims(head, tail, axis):
-    count = lax.axis_size(axis)
-    ends = count - 1
-    return (
-        lax.ppermute(tail, axis, [(i, i + 1) for i in range(ends)]),
-        lax.ppermute(head, axis, [(i + 1, i) for i in range(ends)]),
-    )
+MESH = pl.DeviceIdType.MESH
+
+
+def greet(row, col, row_peers, col_peers):
+    barrier = pltpu.get_barrier_semaphore()
+    for peer in row_peers:
+        pl.semaphore_signal(barrier, inc=1, device_id=(peer, col), device_id_type=MESH)
+    for peer in col_peers:
+        pl.semaphore_signal(barrier, inc=1, device_id=(row, peer), device_id_type=MESH)
+    pl.semaphore_wait(barrier, len(row_peers) + len(col_peers))
+
+
+def rim_copies(row, col, n_row, head, tail, below, above, send, recv):
+    up = pltpu.make_async_remote_copy(
+        src_ref=tail,
+        dst_ref=above,
+        send_sem=send.at[0],
+        recv_sem=recv.at[0],
+        device_id=(lax.rem(row + 1, n_row), col),
+        device_id_type=MESH,
+    )
+    down = pltpu.make_async_remote_copy(
+        src_ref=head,
+        dst_ref=below,
+        send_sem=send.at[1],
+        recv_sem=recv.at[1],
+        device_id=(lax.rem(row + n_row - 1, n_row), col),
+        device_id_type=MESH,
+    )
+    return up, down
+
+
+def start_rims(row, n_row, up, down):
+    pl.when(row < n_row - 1)(lambda: up.start())
+    pl.when(row > 0)(lambda: down.start())
+
+
+def finish_rims(row, n_row, up, down):
+    @pl.when(row < n_row - 1)
+    def _():
+        up.wait_send()
+        down.wait_recv()
+
+    @pl.when(row > 0)
+    def _():
+        down.wait_send()
+        up.wait_recv()
+
+
+def entry_kernel(
+    n_row, n_col, own, hub, lower, upper, hubs, own_sem, rim_send, rim_recv, hub_send, hub_recv
+):
+    row, col = lax.axis_index("row"), lax.axis_index("col")
+    nodes, share = own.shape[0], hub.shape[0]
+    peers = [lax.rem(col + k, n_col) for k in range(1, n_col)]
+    greet(row, col, [lax.rem(row + k, n_row) for k in range(1, n_row)], peers)
+    up, down = rim_copies(
+        row,
+        col,
+        n_row,
+        own.at[pl.ds(0, HALO)],
+        own.at[pl.ds(nodes - HALO, HALO)],
+        upper,
+        lower,
+        rim_send,
+        rim_recv,
+    )
+    start_rims(row, n_row, up, down)
+    mine = hubs.at[pl.ds(pl.multiple_of(col * share, share), share)]
+    copies = [
+        pltpu.make_async_remote_copy(
+            src_ref=hub,
+            dst_ref=mine,
+            send_sem=hub_send.at[k],
+            recv_sem=hub_recv.at[k],
+            device_id=(row, peer),
+            device_id_type=MESH,
+        )
+        for k, peer in enumerate(peers)
+    ]
+    for copy in copies:
+        copy.start()
+    kept = pltpu.make_async_copy(hub, mine, own_sem)
+    kept.start()
+    kept.wait()
+    for copy in copies:
+        copy.wait()
+    finish_rims(row, n_row, up, down)
+
+
+def entry_exchange(features, hub_local, n_row, n_col):
+    width = features.shape[1]
+    share = hub_local.shape[0]
+    anywhere = pl.BlockSpec(memory_space=pl.ANY)
+    dma = pltpu.SemaphoreType.DMA
+    return pl.pallas_call(
+        functools.partial(entry_kernel, n_row, n_col),
+        out_shape=(
+            jax.ShapeDtypeStruct((HALO, width), jnp.bfloat16),
+            jax.ShapeDtypeStruct((HALO, width), jnp.bfloat16),
+            jax.ShapeDtypeStruct((n_col * share, width), jnp.bfloat16),
+        ),
+        in_specs=[anywhere] * 2,
+        out_specs=(anywhere,) * 3,
+        scratch_shapes=[dma, dma((2,)), dma((2,)), dma((n_col - 1,)), dma((n_col - 1,))],
+        compiler_params=pltpu.CompilerParams(collective_id=0, has_side_effects=True),
+        name="entry_exchange",
+    )(features, hub_local)
+
+
+def exit_kernel(
+    n_row,
+    n_col,
+    border,
+    hub,
+    grads,
+    rim,
+    hub_total,
+    weights,
+    bias,
+    hub_in,
+    col_in,
+    row_in,
+    rim_send,
+    rim_recv,
+    hub_send,
+    hub_recv,
+    col_send,
+    col_recv,
+    row_send,
+    row_recv,
+    out_send,
+    out_recv,
+):
+    row, col = lax.axis_index("row"), lax.axis_index("col")
+    share = hub_total.shape[0]
+    part = weights.shape[1]
+    peers = [lax.rem(col + k, n_col) for k in range(1, n_col)]
+    row_peers = [lax.rem(row + k, n_row) for k in range(1, n_row)]
+    greet(row, col, row_peers, peers)
+
+    def remote(src, dst, send, recv, device):
+        return pltpu.make_async_remote_copy(
+            src_ref=src,
+            dst_ref=dst,
+            send_sem=send,
+            recv_sem=recv,
+            device_id=device,
+            device_id_type=MESH,
+        )
+
+    first = [
+        remote(grads.at[peer], col_in.at[col], col_send.at[k], col_recv.at[k], (row, peer))
+        for k, peer in enumerate(peers)
+    ]
+    for copy in first:
+        copy.start()
+    up, down = rim_copies(
+        row,
+        col,
+        n_row,
+        border.at[pl.ds(0, HALO)],
+        border.at[pl.ds(HALO, HALO)],
+        rim.at[pl.ds(HALO, HALO)],
+        rim.at[pl.ds(0, HALO)],
+        rim_send,
+        rim_recv,
+    )
+    start_rims(row, n_row, up, down)
+    sends = [
+        remote(
+            hub.at[pl.ds(pl.multiple_of(peer * share, share), share)],
+            hub_in.at[col],
+            hub_send.at[k],
+            hub_recv.at[k],
+            (row, peer),
+        )
+        for k, peer in enumerate(peers)
+    ]
+    for copy in sends:
+        copy.start()
+
+    @pl.when(row == 0)
+    def _():
+        rim[:HALO, :] = jnp.zeros((HALO, rim.shape[1]), rim.dtype)
+
+    @pl.when(row == n_row - 1)
+    def _():
+        rim[HALO:, :] = jnp.zeros((HALO, rim.shape[1]), rim.dtype)
+
+    col_in[col] = grads[col]
+    for copy in first:
+        copy.wait()
+    total = col_in[0]
+    for k in range(1, n_col):
+        total = total + col_in[k]
+    row_in[row] = total
+    second = [
+        remote(row_in.at[row], row_in.at[row], row_send.at[k], row_recv.at[k], (peer, col))
+        for k, peer in enumerate(row_peers)
+    ]
+    for copy in second:
+        copy.start()
+    hub_in[col] = hub[pl.ds(pl.multiple_of(col * share, share), share), :]
+    for copy in second:
+        copy.wait()
+    total = row_in[0]
+    for k in range(1, n_row):
+        total = total + row_in[k]
+    weights[col] = total[:part]
+    bias[...] = jnp.sum(total[part:], axis=0, keepdims=True)
+    third = [
+        remote(weights.at[col], weights.at[col], out_send.at[k], out_recv.at[k], (row, peer))
+        for k, peer in enumerate(peers)
+    ]
+    for copy in third:
+        copy.start()
+    for copy in sends:
+        copy.wait()
+    shared = hub_in[0].astype(jnp.float32)
+    for k in range(1, n_col):
+        shared = shared + hub_in[k].astype(jnp.float32)
+    hub_total[...] = shared
+    for copy in third:
+        copy.wait()
+    finish_rims(row, n_row, up, down)
+
+
+def exit_exchange(border, hub, grads, n_row, n_col):
+    width = border.shape[1]
+    share = hub.shape[0] // n_col
+    part, hidden = grads.shape[1] - 8, grads.shape[2]
+    vmem = pl.BlockSpec(memory_space=pltpu.VMEM)
+    dma = pltpu.SemaphoreType.DMA
+    return pl.pallas_call(
+        functools.partial(exit_kernel, n_row, n_col),
+        out_shape=(
+            jax.ShapeDtypeStruct(border.shape, jnp.bfloat16),
+            jax.ShapeDtypeStruct((share, width), jnp.float32),
+            jax.ShapeDtypeStruct((n_col, part, hidden), jnp.float32),
+            jax.ShapeDtypeStruct((1, hidden), jnp.float32),
+        ),
+        in_specs=[vmem] * 3,
+        out_specs=(vmem,) * 4,
+        scratch_shapes=[
+            pltpu.VMEM((n_col, share, width), jnp.bfloat16),
+            pltpu.VMEM(grads.shape, jnp.float32),
+            pltpu.VMEM((n_row,) + grads.shape[1:], jnp.float32),
+            dma((2,)),
+            dma((2,)),
+        ]
+        + [dma((n_col - 1,))] * 4
+        + [dma((n_row - 1,))] * 2
+        + [dma((n_col - 1,))] * 2,
+        compiler_params=pltpu.CompilerParams(
+            collective_id=1, has_side_effects=True, vmem_limit_bytes=VMEM_LIMIT
+        ),
+        name="exit_exchange",
+    )(border, hub, grads)
+
+
+def finish_kernel(hub_rows, own, dz, w_self, rim, hub, out, total):
+    chunk = 512
+    nodes = own.shape[0]
+
+    def back(i, carry):
+        at = pl.ds(pl.multiple_of(i * chunk, chunk), chunk)
+        total[at, :] = own[at, :] + lax.dot_general(
+            dz[at, :], w_self[...], (((1,), (1,)), ((), ())), preferred_element_type=jnp.float32
+        )
+        return carry
+
+    lax.fori_loop(0, nodes // chunk, back, 0)
+    total[:HALO, :] += rim[:HALO, :].astype(jnp.float32)
+    total[nodes - HALO :, :] += rim[HALO:, :].astype(jnp.float32)
+
+    def add(i, carry):
+        for u in range(UNROLL):
+            k = i * UNROLL + u
+            at = pl.ds(hub_rows[k], 1)
+            total[at, :] += hub[pl.ds(k, 1), :]
+        return carry
+
+    lax.fori_loop(0, hub.shape[0] // UNROLL, add, 0)
+    out[...] = total[...].astype(out.dtype)
+
+
+def finish(hub_rows, own, dz, w_self, rim, hub):
+    vmem = pl.BlockSpec(memory_space=pltpu.VMEM)
+    return pl.pallas_call(
+        finish_kernel,
+        out_shape=jax.ShapeDtypeStruct(own.shape, jnp.bfloat16),
+        in_specs=[pl.BlockSpec(memory_space=pltpu.SMEM)] + [vmem] * 5,
+        out_specs=vmem,
+        scratch_shapes=[pltpu.VMEM(own.shape, jnp.float32)],
+        compiler_params=pltpu.CompilerParams(vmem_limit_bytes=VMEM_LIMIT),
+        name="finish",
+    )(hub_rows, own, dz, w_self, rim, hub)
 
 
 def gelu_tanh(value):
@@ -134,9 +425,9 @@
 
 def on_device(features, neighbors, counts, hub_rows, w_self, w_neigh, out_bias, cotangent):
     node_count = features.shape[0]
-    lower, upper = rims(features[:HALO], features[node_count - HALO :], "row")
+    n_row, n_col = lax.axis_size("row"), lax.axis_size("col")
     hub_local = jnp.take(features, hub_rows, axis=0)
-    hub_table = lax.all_gather(hub_local, "col", axis=0, tiled=True)
+    lower, upper, hub_table = entry_exchange(features, hub_local, n_row, n_col)
     hubs = hub_table.shape[0]
     extent = 2 * HALO + node_count + hubs
     active = jnp.arange(FANOUT)[:, None] < counts[None, :]
@@ -158,16 +449,13 @@
     grad_neigh = lax.dot_general(agg, dz, dims, preferred_element_type=jnp.float32)
     source = lax.dot_general(dz, w_neigh, back_dims, preferred_element_type=jnp.float32) / divisor
     mine, border, hub_grads = scatter_sum(rows, source, hubs)
-    from_above, from_below = rims(border[:HALO], border[HALO:], "row")
-    mine = mine.at[:HALO].add(from_above.astype(jnp.float32))
-    mine = mine.at[node_count - HALO :].add(from_below.astype(jnp.float32))
-    hub_share = lax.psum_scatter(hub_grads, "col", scatter_dimension=0, tiled=True).astype(
-        jnp.float32
-    )
-    mine = mine.at[hub_rows].add(hub_share)
-    local_grad = lax.dot_general(dz, w_self, back_dims, preferred_element_type=jnp.float32)
-    grad_features = (local_grad + mine).astype(jnp.bfloat16)
-    grad_self, grad_neigh, grad_b = lax.psum((grad_self, grad_neigh, grad_b), ("row", "col"))
+    hidden = dz.shape[1]
+    blocks = jnp.concatenate([grad_self, grad_neigh], axis=0).reshape(n_col, -1, hidden)
+    grads = jnp.concatenate([blocks, jnp.broadcast_to(jnp.pad(grad_b[None, :], ((0, 7), (0, 0))), (n_col, 8, hidden))], axis=1)
+    rim, hub_share, weights, bias = exit_exchange(border, hub_grads, grads, n_row, n_col)
+    grad_features = finish(hub_rows, mine, dz, w_self, rim, hub_share)
+    weights = weights.reshape(2, -1, hidden)
+    grad_self, grad_neigh, grad_b = weights[0], weights[1], bias[0]
     return (activations, grad_features, grad_self, grad_neigh, grad_b)
 
 

time: 318 us -> 174 us (0.55)
  waiting for transfers between devices: 81.5 us -> 0 us
  blocking collectives: 51.5 us -> 0 us
  Pallas kernels: 115 us -> 153 us
  between operations: 15.6 us -> 0.77 us
  starting transfers between devices: 11.7 us -> 0 us
  other arithmetic: 16.7 us -> 7.18 us
  matrix products: 17.3 us -> 8.61 us
  local copies, waits for them, and re-layouts: 8.09 us -> 4.22 us
    psum x1 -> x0, waiting for transfers between devices: 81.4 us -> none  [on_device(): lax.psum((grad_self, grad_neigh, grad_b), ('row', 'col'))]
    psum x1 -> x0, blocking collectives: 40.8 us -> none  [on_device(): lax.psum((grad_self, grad_neigh, grad_b), ('row', 'col'))]
    pallas_call x0 -> x3, Pallas kernels: none -> 38.8 us  [the longest x1 20.4 us: exit_exchange(): pl.pallas_call(functools.partial(exit_kernel, n_row, n_col), out_shape=(j...]
    ppermute x4 -> x0, starting transfers between devices: 11.6 us -> none  [the longest x2 9.05 us: rims(): lax.ppermute(tail, axis, [(i, i + 1) for i in range(ends)])]
    all_gather x1 -> x0, blocking collectives: 10.8 us -> none  [on_device(): hub_table = lax.all_gather(hub_local, 'col', axis=0, tiled=True)]
    scatter-add x3 -> x0, other arithmetic: 8.05 us -> none  [the longest x1 4.29 us: on_device(): mine = mine.at[hub_rows].add(hub_share)]
    dot_general x1 -> x0, matrix products: 3.61 us -> none  [on_device(): lax.dot_general(dz, w_self, back_dims, preferred_element_type=jnp.float32)]
  transfers between devices with their start and end apart: 6 -> 0, of which waited for: 1 -> 0; matrix products, arithmetic and copies ran while one was open for 6% -> 0% of each run, Pallas kernels for 0% -> 0%
where the time goes in v2:
time: 174 us
  Pallas kernels  153 us (88%)
  matrix products  8.61 us (5%)
  other arithmetic  7.18 us (4%)
  local copies, waits for them, and re-layouts  4.22 us (2%)
    pallas_call x1, Pallas kernels, scatter_sum(): pl.pallas_call(scatter_kernel, out_shape=(jax.ShapeDtypeStruct((nodes, wi...  59.2 us
    pallas_call x1, Pallas kernels, gather_sum(): pl.pallas_call(gather_kernel, out_shape=jax.ShapeDtypeStruct(own.shape, j...  55.2 us
    pallas_call x1, Pallas kernels, exit_exchange(): pl.pallas_call(functools.partial(exit_kernel, n_row, n_col), out_shape=(j...  20.4 us
    pallas_call x1, Pallas kernels, entry_exchange(): pl.pallas_call(functools.partial(entry_kernel, n_row, n_col), out_shape=(...  12.6 us
    pallas_call x1, Pallas kernels, finish(): pl.pallas_call(finish_kernel, out_shape=jax.ShapeDtypeStruct(own.shape, j...  5.76 us
    dot_general x1, matrix products, on_device(): jnp.dot(agg, w_neigh, preferred_element_type=jnp.float32)  4.97 us

profile of v2, /device:TPU:0, one launch (start us, length us, event | category | flops | bytes accessed | tf_op | source)
XLA Modules:
  0.0 174.0 jit_solution(4526323155988974434)
XLA Ops:
  0.6 0.0 copy-start
  0.6 0.7 compare_and_fusion
  1.3 0.7 compare_select_fusion
  2.0 0.7 convert_element_type.20
  2.7 2.0 %gather_fusion = bf16[128,128]{1,0:T(8,128)(2,1)S(1)} fusion(bf16[4096,128]{1,0:T(8,128)(2,1)} %own_ref.1, s32[1024]{0:T(1024)S(1)} %pad_clamp_fusion), kind=kCustom, calls=%fused_computation | custom fusion | bytes 66048 | tf_op jit(solution)/shard_map/jit(_take)/gather | solution.py:429
  4.7 0.7 broadcast_select_fusion.hub
  5.4 1.7 bitcast_select_fusion.rows_ref
  7.1 12.6 %entry_exchange.1 = (bf16[1024,128]{1,0:T(8,128)(2,1)}, bf16[1024,128]{1,0:T(8,128)(2,1)}, bf16[1024,128]{1,0:T(8,128)(2,1)}) custom-call(bf16[4096,128]{1,0:T(8,128)(2,1)} %own_ref.1, bf16[128,128]{1,0:T(8,128)(2,1)} %broadcast_select_fusion.hub), custom_call_target="tpu_custom_call" | custom-call | tf_op jit(solution)/shard_map/entry_exchange/pallas_call | solution.py:217
  19.7 55.2 %gather_sum.1 = f32[4096,128]{1,0:T(8,128)} custom-call(s32[10,4096]{1,0:T(8,128)} %bitcast_select_fusion.rows_ref, bf16[1024,128]{1,0:T(8,128)(2,1)} %get-tuple-element.15.lower_ref, bf16[4096,128]{1,0:T(8,128)(2,1)} %own_ref.1, bf16[1024,128]{1,0:T(8,128)(2,1)} %get-tuple-element.16.upper_ref, bf16[1024,128]{1,0:T(8,128)(2,1)} %get-tuple-element.17.hub_ref), custom_call_target="tpu_custom_call" | custom-call | tf_op jit(solution)/shard_map/gather_sum/pallas_call | solution.py:42
  74.9 1.9 %divide_convert_fusion = bf16[4096,128]{1,0:T(8,128)(2,1)S(1)} fusion(f32[4096,128]{1,0:T(8,128)} %gather_sum.1, f32[4096]{0:T(1024)S(1)} %convert_element_type.20), kind=kLoop, calls=%fused_computation.20 | loop fusion | flops 1048576 | bytes 3162112 | tf_op jit(solution)/shard_map/convert_element_type | solution.py:436
  76.8 0.0 copy-start.6
  76.9 0.0 copy-start.7
  76.9 0.7 fusion.13
  77.6 0.9 copy-done.6
  78.4 5.0 %convert_reduce_fusion = (f32[256]{0:T(256)S(1)}, bf16[4096,256]{1,0:T(8,128)(2,1)S(1)}, bf16[4096,256]{1,0:T(8,128)(2,1)}) fusion(bf16[4096,256]{1,0:T(8,128)(2,1)S(1)} %copy-done.6, f32[256]{0:T(256)S(1)} %copy-done.7, f32[4096,256]{1,0:T(8,128)S(1)} %fusion.13, bf16[4096,128]{1,0:T(8,128)(2,1)S(1)} %divide_convert_fusion, bf16[128,256]{1,0:T(8,128)(2,1)S(1)} %copy-done), kind=kOutput, calls=%fused_computation.18 | convolution fusion | flops 296746752 | bytes 11601920 | tf_op jit(solution)/shard_map/dot_general | solution.py:439
  83.4 0.5 fusion.14
  84.0 0.6 convolution_bitcast_fusion
  84.5 0.8 pad_maximum_fusion.grads
  85.3 1.9 %convolution_divide_fusion.source_ref = f32[4096,128]{1,0:T(8,128)} fusion(bf16[4096,256]{1,0:T(8,128)(2,1)S(1)} %get-tuple-element.26.dz, bf16[128,256]{1,0:T(8,128)(2,1)S(1)} %copy-done, f32[4096]{0:T(1024)S(1)} %convert_element_type.20), kind=kOutput, calls=%fused_computation.7 | convolution fusion | flops 268959744 | bytes 4276224 | tf_op jit(solution)/shard_map/dot_general | solution.py:450
  87.2 59.2 %scatter_sum.1 = (f32[4096,128]{1,0:T(8,128)}, bf16[2048,128]{1,0:T(8,128)(2,1)}, bf16[1024,128]{1,0:T(8,128)(2,1)}) custom-call(s32[10,4096]{1,0:T(8,128)} %bitcast_select_fusion.rows_ref, f32[4096,128]{1,0:T(8,128)} %convolution_divide_fusion.source_ref), custom_call_target="tpu_custom_call" | custom-call | tf_op jit(solution)/shard_map/scatter_sum/pallas_call | solution.py:107
  146.4 20.4 %exit_exchange.1 = (bf16[2048,128]{1,0:T(8,128)(2,1)}, f32[128,128]{1,0:T(8,128)}, f32[8,32,256]{2,1,0:T(8,128)}, f32[1,256]{1,0:T(1,128)}) custom-call(bf16[2048,128]{1,0:T(8,128)(2,1)} %get-tuple-element.19.border, bf16[1024,128]{1,0:T(8,128)(2,1)} %get-tuple-element.20.hub, f32[8,40,256]{2,1,0:T(8,128)} %pad_maximum_fusion.grads), custom_call_target="tpu_custom_call" | custom-call | tf_op jit(solution)/shard_map/exit_exchange/pallas_call | solution.py:356
  166.9 5.8 %finish.1 = bf16[4096,128]{1,0:T(8,128)(2,1)} custom-call(s32[128]{0:T(128)} %hub_rows.1, f32[4096,128]{1,0:T(8,128)} %get-tuple-element.18.own, bf16[4096,256]{1,0:T(8,128)(2,1)} %copy-done.2, bf16[128,256]{1,0:T(8,128)(2,1)} %w_self.1, bf16[2048,128]{1,0:T(8,128)(2,1)} %get-tuple-element.21.rim, f32[128,128]{1,0:T(8,128)} %get-tuple-element.22.hub), custom_call_target="tpu_custom_call" | custom-call | tf_op jit(solution)/shard_map/finish/pallas_call | solution.py:411
  172.7 0.7 fusion.12
  173.4 0.6 copy.14
  (16 shorter events, 0.1 us)
Async XLA Ops:
  0.6 76.9 %copy-start = (bf16[128,256]{1,0:T(8,128)(2,1)S(1)}, bf16[128,256]{1,0:T(8,128)(2,1)}, u32[]{:S(2)}) copy-start(bf16[128,256]{1,0:T(8,128)(2,1)} %param.13) | copy-start | bytes 196612
  7.1 69.7 %copy-start.1 = (bf16[4096,128]{1,0:T(8,128)(2,1)S(1)}, bf16[4096,128]{1,0:T(8,128)(2,1)}, u32[]{:S(2)}) copy-start(bf16[4096,128]{1,0:T(8,128)(2,1)} %own_ref.1) | copy-start | bytes 3145732
  7.1 69.7 %copy-start.3 = (bf16[128,256]{1,0:T(8,128)(2,1)S(1)}, bf16[128,256]{1,0:T(8,128)(2,1)}, u32[]{:S(2)}) copy-start(bf16[128,256]{1,0:T(8,128)(2,1)} %w_self.1) | copy-start | bytes 196612
  76.8 1.6 copy-start.6
  76.9 1.6 copy-start.7
  83.4 3.8 %copy-start.2 = (bf16[4096,256]{1,0:T(8,128)(2,1)}, bf16[4096,256]{1,0:T(8,128)(2,1)S(1)}, u32[]{:S(2)}) copy-start(bf16[4096,256]{1,0:T(8,128)(2,1)S(1)} %get-tuple-element.26.dz) | copy-start | bytes 6291460
  166.9 5.8 %copy-start.4 = (f32[8,32,256]{2,1,0:T(8,128)S(1)}, f32[8,32,256]{2,1,0:T(8,128)}, u32[]{:S(2)}) copy-start(f32[8,32,256]{2,1,0:T(8,128)} %get-tuple-element.23) | copy-start | bytes 786436
  166.9 6.5 %copy-start.5 = (f32[1,256]{1,0:T(1,128)S(1)}, f32[1,256]{1,0:T(1,128)}, u32[]{:S(2)}) copy-start(f32[1,256]{1,0:T(1,128)} %get-tuple-element.24) | copy-start | bytes 3076

commit v3 on v2

--- a/solution.py
+++ b/solution.py
@@ -10,47 +10,63 @@
 FANOUT = 10
 HALO = 1024
 UNROLL = 8
-PAD = 8
 VMEM_LIMIT = 60 * 1024 * 1024
 
 
-def gather_kernel(rows_ref, lower_ref, own_ref, upper_ref, hub_ref, total_ref, table):
+def by_count(starts_ref, order_ref, visit):
+    for live in range(1, FANOUT + 1):
+        first, last = starts_ref[live - 1], starts_ref[live]
+        groups = lax.div(last - first, UNROLL)
+
+        def group(i, carry, first=first, live=live):
+            at = first + i * UNROLL
+            visit([order_ref[at + u] for u in range(UNROLL)], live)
+            return carry
+
+        def single(i, carry, live=live):
+            visit([order_ref[i]], live)
+            return carry
+
+        lax.fori_loop(0, groups, group, 0)
+        lax.fori_loop(first + groups * UNROLL, last, single, 0)
+
+
+def gather_kernel(
+    rows_ref, starts_ref, order_ref, lower_ref, own_ref, upper_ref, hub_ref, total_ref, table
+):
     at = 0
     for part in (lower_ref, own_ref, upper_ref, hub_ref):
         size = part.shape[0]
         table[at : at + size, :] = part[...].astype(jnp.float32)
         at += size
-    table[at : at + PAD, :] = jnp.zeros((PAD, table.shape[1]), jnp.float32)
-
-    def step(i, carry):
-        for u in range(UNROLL):
-            n = i * UNROLL + u
-            picked = [table[pl.ds(rows_ref[s, n], 1), :] for s in range(FANOUT)]
+
+    def visit(nodes, live):
+        for n in nodes:
+            picked = [table[pl.ds(rows_ref[s, n], 1), :] for s in range(live)]
             while len(picked) > 1:
                 picked = [a + b for a, b in zip(picked[::2], picked[1::2])] + (
                     [picked[-1]] if len(picked) % 2 else []
                 )
             total_ref[pl.ds(n, 1), :] = picked[0]
-        return carry
-
-    lax.fori_loop(0, total_ref.shape[0] // UNROLL, step, 0)
-
-
-def gather_sum(rows, lower, own, upper, hubs):
+
+    by_count(starts_ref, order_ref, visit)
+
+
+def gather_sum(rows, starts, order, lower, own, upper, hubs):
     extent = lower.shape[0] + own.shape[0] + upper.shape[0] + hubs.shape[0]
     vmem = pl.BlockSpec(memory_space=pltpu.VMEM)
     return pl.pallas_call(
         gather_kernel,
         out_shape=jax.ShapeDtypeStruct(own.shape, jnp.float32),
-        in_specs=[pl.BlockSpec(memory_space=pltpu.SMEM)] + [vmem] * 4,
+        in_specs=[pl.BlockSpec(memory_space=pltpu.SMEM)] * 3 + [vmem] * 4,
         out_specs=vmem,
-        scratch_shapes=[pltpu.VMEM((extent + PAD, own.shape[1]), jnp.float32)],
+        scratch_shapes=[pltpu.VMEM((extent, own.shape[1]), jnp.float32)],
         compiler_params=pltpu.CompilerParams(vmem_limit_bytes=VMEM_LIMIT),
         name="gather_sum",
-    )(rows, lower, own, upper, hubs)
-
-
-def scatter_kernel(rows_ref, source_ref, own_ref, border_ref, hub_ref, *sums):
+    )(rows, starts, order, lower, own, upper, hubs)
+
+
+def scatter_kernel(rows_ref, starts_ref, order_ref, source_ref, own_ref, border_ref, hub_ref, *sums):
     chunk = 512
     extent = sums[0].shape[0]
     width = sums[0].shape[1]
@@ -65,18 +81,17 @@
 
     lax.fori_loop(0, extent // chunk, clear, 0)
 
-    def step(i, carry):
-        for u in range(UNROLL):
-            n = i * UNROLL + u
-            value = source_ref[pl.ds(n, 1), :]
-            for first in range(0, FANOUT, kinds):
-                rows = [rows_ref[first + k, n] for k in range(kinds)]
-                held = [sums[k][pl.ds(rows[k], 1), :] for k in range(kinds)]
-                for k in range(kinds):
-                    sums[k][pl.ds(rows[k], 1), :] = held[k] + value
-        return carry
-
-    lax.fori_loop(0, source_ref.shape[0] // UNROLL, step, 0)
+    def visit(nodes, live):
+        values = [source_ref[pl.ds(n, 1), :] for n in nodes]
+        edges = [(u, s) for u in range(len(nodes)) for s in range(live)]
+        for first in range(0, len(edges), kinds):
+            batch = edges[first : first + kinds]
+            rows = [rows_ref[s, nodes[u]] for u, s in batch]
+            held = [sums[k][pl.ds(row, 1), :] for k, row in enumerate(rows)]
+            for k, (u, s) in enumerate(batch):
+                sums[k][pl.ds(rows[k], 1), :] = held[k] + values[u]
+
+    by_count(starts_ref, order_ref, visit)
 
     def added(at, size):
         total = sums[0][pl.ds(at, size), :]
@@ -99,7 +114,7 @@
     emit(hub_ref, 0, 2 * HALO + nodes, hub_ref.shape[0])
 
 
-def scatter_sum(rows, source, hubs):
+def scatter_sum(rows, starts, order, source, hubs):
     nodes, width = source.shape
     extent = 2 * HALO + nodes + hubs
     kinds = 10 if extent <= 8192 else 5
@@ -111,12 +126,12 @@
             jax.ShapeDtypeStruct((2 * HALO, width), jnp.bfloat16),
             jax.ShapeDtypeStruct((hubs, width), jnp.bfloat16),
         ),
-        in_specs=[pl.BlockSpec(memory_space=pltpu.SMEM), vmem],
+        in_specs=[pl.BlockSpec(memory_space=pltpu.SMEM)] * 3 + [vmem],
         out_specs=(vmem, vmem, vmem),
-        scratch_shapes=[pltpu.VMEM((extent + PAD, width), jnp.float32)] * kinds,
+        scratch_shapes=[pltpu.VMEM((extent, width), jnp.float32)] * kinds,
         compiler_params=pltpu.CompilerParams(vmem_limit_bytes=VMEM_LIMIT),
         name="scatter_sum",
-    )(rows, source)
+    )(rows, starts, order, source)
 
 
 MESH = pl.DeviceIdType.MESH
@@ -169,7 +184,21 @@
 
 
 def entry_kernel(
-    n_row, n_col, own, hub, lower, upper, hubs, own_sem, rim_send, rim_recv, hub_send, hub_recv
+    n_row,
+    n_col,
+    hub_rows,
+    own,
+    lower,
+    upper,
+    hubs,
+    wide,
+    picked,
+    hub,
+    own_sem,
+    rim_send,
+    rim_recv,
+    hub_send,
+    hub_recv,
 ):
     row, col = lax.axis_index("row"), lax.axis_index("col")
     nodes, share = own.shape[0], hub.shape[0]
@@ -187,6 +216,16 @@
         rim_recv,
     )
     start_rims(row, n_row, up, down)
+    wide[...] = own[...].astype(jnp.float32)
+
+    def pick(i, carry):
+        for u in range(UNROLL):
+            k = i * UNROLL + u
+            picked[pl.ds(k, 1), :] = wide[pl.ds(hub_rows[k], 1), :]
+        return carry
+
+    lax.fori_loop(0, share // UNROLL, pick, 0)
+    hub[...] = picked[...].astype(jnp.bfloat16)
     mine = hubs.at[pl.ds(pl.multiple_of(col * share, share), share)]
     copies = [
         pltpu.make_async_remote_copy(
@@ -209,9 +248,9 @@
     finish_rims(row, n_row, up, down)
 
 
-def entry_exchange(features, hub_local, n_row, n_col):
+def entry_exchange(features, hub_rows, n_row, n_col):
     width = features.shape[1]
-    share = hub_local.shape[0]
+    share = hub_rows.shape[0]
     anywhere = pl.BlockSpec(memory_space=pl.ANY)
     dma = pltpu.SemaphoreType.DMA
     return pl.pallas_call(
@@ -221,12 +260,26 @@
             jax.ShapeDtypeStruct((HALO, width), jnp.bfloat16),
             jax.ShapeDtypeStruct((n_col * share, width), jnp.bfloat16),
         ),
-        in_specs=[anywhere] * 2,
+        in_specs=[
+            pl.BlockSpec(memory_space=pltpu.SMEM),
+            pl.BlockSpec(memory_space=pltpu.VMEM),
+        ],
         out_specs=(anywhere,) * 3,
-        scratch_shapes=[dma, dma((2,)), dma((2,)), dma((n_col - 1,)), dma((n_col - 1,))],
-        compiler_params=pltpu.CompilerParams(collective_id=0, has_side_effects=True),
+        scratch_shapes=[
+            pltpu.VMEM(features.shape, jnp.float32),
+            pltpu.VMEM((share, width), jnp.float32),
+            pltpu.VMEM((share, width), jnp.bfloat16),
+            dma,
+            dma((2,)),
+            dma((2,)),
+            dma((n_col - 1,)),
+            dma((n_col - 1,)),
+        ],
+        compiler_params=pltpu.CompilerParams(
+            collective_id=0, has_side_effects=True, vmem_limit_bytes=VMEM_LIMIT
+        ),
         name="entry_exchange",
-    )(features, hub_local)
+    )(hub_rows, features)
 
 
 def exit_kernel(
@@ -426,14 +479,16 @@
 def on_device(features, neighbors, counts, hub_rows, w_self, w_neigh, out_bias, cotangent):
     node_count = features.shape[0]
     n_row, n_col = lax.axis_size("row"), lax.axis_size("col")
-    hub_local = jnp.take(features, hub_rows, axis=0)
-    lower, upper, hub_table = entry_exchange(features, hub_local, n_row, n_col)
+    lower, upper, hub_table = entry_exchange(features, hub_rows, n_row, n_col)
     hubs = hub_table.shape[0]
-    extent = 2 * HALO + node_count + hubs
-    active = jnp.arange(FANOUT)[:, None] < counts[None, :]
-    rows = jnp.where(active, neighbors.T, extent)
+    rows = neighbors.T
+    keys = counts * node_count + jnp.arange(node_count, dtype=jnp.int32)
+    order = lax.sort(keys, is_stable=False) % node_count
+    starts = jnp.sum(
+        counts[None, :] <= jnp.arange(FANOUT + 1)[:, None], axis=1, dtype=jnp.int32
+    )
     divisor = counts.astype(jnp.float32)[:, None]
-    agg = (gather_sum(rows, lower, features, upper, hub_table) / divisor).astype(jnp.bfloat16)
+    agg = (gather_sum(rows, starts, order, lower, features, upper, hub_table) / divisor).astype(jnp.bfloat16)
     pre = (
         jnp.dot(features, w_self, preferred_element_type=jnp.float32)
         + jnp.dot(agg, w_neigh, preferred_element_type=jnp.float32)
@@ -448,7 +503,7 @@
     grad_b = jnp.sum(dz.astype(jnp.float32), axis=0)
     grad_neigh = lax.dot_general(agg, dz, dims, preferred_element_type=jnp.float32)
     source = lax.dot_general(dz, w_neigh, back_dims, preferred_element_type=jnp.float32) / divisor
-    mine, border, hub_grads = scatter_sum(rows, source, hubs)
+    mine, border, hub_grads = scatter_sum(rows, starts, order, source, hubs)
     hidden = dz.shape[1]
     blocks = jnp.concatenate([grad_self, grad_neigh], axis=0).reshape(n_col, -1, hidden)
     grads = jnp.concatenate([blocks, jnp.broadcast_to(jnp.pad(grad_b[None, :], ((0, 7), (0, 0))), (n_col, 8, hidden))], axis=1)

time: 174 us -> 147 us (0.84)
  Pallas kernels: 153 us -> 124 us
  other arithmetic: 7.18 us -> 10.5 us
  local copies, waits for them, and re-layouts: 4.22 us -> 2.21 us
    pallas_call x1, Pallas kernels: 59.2 us -> 44.1 us  [scatter_sum(): pl.pallas_call(scatter_kernel, out_shape=(jax.ShapeDtypeStruct((nodes, wi...]
    pallas_call x1, Pallas kernels: 55.2 us -> 40.8 us  [gather_sum(): pl.pallas_call(gather_kernel, out_shape=jax.ShapeDtypeStruct(own.shape, j...]
    sort x0 -> x1, other arithmetic: none -> 4.92 us  [on_device(): order = lax.sort(keys, is_stable=False) % node_count]
    select_n x3 -> x1, other arithmetic: 3.04 us -> 0.64 us  [on_device(): order = lax.sort(keys, is_stable=False) % node_count]
    gather x1 -> x0, local copies, waits for them, and re-layouts: 2.01 us -> none  [on_device(): hub_local = jnp.take(features, hub_rows, axis=0)]
where the time goes in v3:
time: 147 us; the launch traced here: 146 us
  Pallas kernels  124 us (84%)
  other arithmetic  10.5 us (7%)
  matrix products  8.61 us (6%)
  local copies, waits for them, and re-layouts  2.21 us (2%)
    pallas_call x1, Pallas kernels, scatter_sum(): pl.pallas_call(scatter_kernel, out_shape=(jax.ShapeDtypeStruct((nodes, wi...  44.1 us
    pallas_call x1, Pallas kernels, gather_sum(): pl.pallas_call(gather_kernel, out_shape=jax.ShapeDtypeStruct(own.shape, j...  40.8 us
    pallas_call x1, Pallas kernels, exit_exchange(): pl.pallas_call(functools.partial(exit_kernel, n_row, n_col), out_shape=(j...  19.6 us
    pallas_call x1, Pallas kernels, entry_exchange(): pl.pallas_call(functools.partial(entry_kernel, n_row, n_col), out_shape=(...  13.7 us
    pallas_call x1, Pallas kernels, finish(): pl.pallas_call(finish_kernel, out_shape=jax.ShapeDtypeStruct(own.shape, j...  5.76 us
    dot_general x1, matrix products, on_device(): jnp.dot(agg, w_neigh, preferred_element_type=jnp.float32)  4.96 us
    sort x1, other arithmetic, on_device(): order = lax.sort(keys, is_stable=False) % node_count  4.92 us

profile of v3, /device:TPU:0, one launch (start us, length us, event | category | flops | bytes accessed | tf_op | source)
XLA Modules:
  0.0 146.0 jit_solution(6048224977609356275)
XLA Ops:
  0.6 0.0 copy-start
  0.6 1.4 convert_reduce_fusion.1.starts_ref
  2.1 0.8 fusion.14
  2.9 4.9 %sort.7 = s32[4096]{0:T(1024)S(1)} sort(s32[4096]{0:T(1024)S(1)} %get-tuple-element.31), dimensions={0}, to_apply=%region_1.2 | sort | flops 49152 | bytes 32768 | tf_op jit(solution)/shard_map/sort | solution.py:486
  7.8 0.6 add_select_fusion.order_ref
  8.4 13.7 %entry_exchange.1 = (bf16[1024,128]{1,0:T(8,128)(2,1)}, bf16[1024,128]{1,0:T(8,128)(2,1)}, bf16[1024,128]{1,0:T(8,128)(2,1)}) custom-call(s32[128]{0:T(128)} %hub_rows.3, bf16[4096,128]{1,0:T(8,128)(2,1)} %own_ref.1), custom_call_target="tpu_custom_call" | custom-call | tf_op jit(solution)/shard_map/entry_exchange/pallas_call | solution.py:256
  22.1 40.8 %gather_sum.1 = f32[4096,128]{1,0:T(8,128)} custom-call(s32[10,4096]{1,0:T(8,128)} %bitcast.19, s32[11]{0:T(128)} %convert_reduce_fusion.1.starts_ref, s32[4096]{0:T(1024)} %add_select_fusion.order_ref, bf16[1024,128]{1,0:T(8,128)(2,1)} %get-tuple-element.15.lower_ref, bf16[4096,128]{1,0:T(8,128)(2,1)} %own_ref.1, ...), custom_call_target="tpu_custom_call" | custom-call | tf_op jit(solution)/shard_map/gather_sum/pallas_call | solution.py:58
  62.9 1.9 %divide_convert_fusion = bf16[4096,128]{1,0:T(8,128)(2,1)S(1)} fusion(f32[4096,128]{1,0:T(8,128)} %gather_sum.1, f32[4096]{0:T(1024)S(1)} %get-tuple-element.30), kind=kLoop, calls=%fused_computation.19 | loop fusion | flops 1048576 | bytes 3162112 | tf_op jit(solution)/shard_map/convert_element_type | solution.py:491
  64.9 0.0 copy-done.1
  64.9 0.0 copy-done.3
  64.9 0.0 copy-start.6
  64.9 0.0 copy-start.7
  64.9 0.7 fusion.15
  65.6 0.9 copy-done.6
  66.5 5.0 %convert_reduce_fusion = (f32[256]{0:T(256)S(1)}, bf16[4096,256]{1,0:T(8,128)(2,1)S(1)}, bf16[4096,256]{1,0:T(8,128)(2,1)}) fusion(bf16[4096,256]{1,0:T(8,128)(2,1)S(1)} %copy-done.6, f32[256]{0:T(256)S(1)} %copy-done.7, f32[4096,256]{1,0:T(8,128)S(1)} %fusion.15, bf16[4096,128]{1,0:T(8,128)(2,1)S(1)} %divide_convert_fusion, bf16[128,256]{1,0:T(8,128)(2,1)S(1)} %copy-done), kind=kOutput, calls=%fused_computation.17 | convolution fusion | flops 296746752 | bytes 11601920 | tf_op jit(solution)/shard_map/dot_general | solution.py:494
  71.5 0.5 fusion.16
  72.0 0.6 convolution_bitcast_fusion
  72.6 0.8 pad_maximum_fusion.grads
  73.4 1.9 %convolution_divide_fusion.source_ref = f32[4096,128]{1,0:T(8,128)} fusion(bf16[4096,256]{1,0:T(8,128)(2,1)S(1)} %get-tuple-element.26.dz, bf16[128,256]{1,0:T(8,128)(2,1)S(1)} %copy-done, f32[4096]{0:T(1024)S(1)} %get-tuple-element.30), kind=kOutput, calls=%fused_computation.6 | convolution fusion | flops 268959744 | bytes 4276224 | tf_op jit(solution)/shard_map/dot_general | solution.py:505
  75.3 44.1 %scatter_sum.1 = (f32[4096,128]{1,0:T(8,128)}, bf16[2048,128]{1,0:T(8,128)(2,1)}, bf16[1024,128]{1,0:T(8,128)(2,1)}) custom-call(s32[10,4096]{1,0:T(8,128)} %bitcast.20, s32[11]{0:T(128)} %convert_reduce_fusion.1.starts_ref, s32[4096]{0:T(1024)} %add_select_fusion.order_ref, f32[4096,128]{1,0:T(8,128)} %convolution_divide_fusion.source_ref), custom_call_target="tpu_custom_call" | custom-call | tf_op jit(solution)/shard_map/scatter_sum/pallas_call | solution.py:122
  119.3 19.6 %exit_exchange.1 = (bf16[2048,128]{1,0:T(8,128)(2,1)}, f32[128,128]{1,0:T(8,128)}, f32[8,32,256]{2,1,0:T(8,128)}, f32[1,256]{1,0:T(1,128)}) custom-call(bf16[2048,128]{1,0:T(8,128)(2,1)} %get-tuple-element.19.border, bf16[1024,128]{1,0:T(8,128)(2,1)} %get-tuple-element.20.hub, f32[8,40,256]{2,1,0:T(8,128)} %pad_maximum_fusion.grads), custom_call_target="tpu_custom_call" | custom-call | tf_op jit(solution)/shard_map/exit_exchange/pallas_call | solution.py:409
  138.9 5.8 %finish.1 = bf16[4096,128]{1,0:T(8,128)(2,1)} custom-call(s32[128]{0:T(128)} %hub_rows.3, f32[4096,128]{1,0:T(8,128)} %get-tuple-element.18.own, bf16[4096,256]{1,0:T(8,128)(2,1)} %copy-done.2, bf16[128,256]{1,0:T(8,128)(2,1)} %w_self.1, bf16[2048,128]{1,0:T(8,128)(2,1)} %get-tuple-element.21.rim, f32[128,128]{1,0:T(8,128)} %get-tuple-element.22.hub), custom_call_target="tpu_custom_call" | custom-call | tf_op jit(solution)/shard_map/finish/pallas_call | solution.py:464
  144.7 0.7 fusion.13
  145.4 0.6 copy.14
  (13 shorter events, 0.1 us)
Async XLA Ops:
  0.6 65.0 %copy-start = (bf16[128,256]{1,0:T(8,128)(2,1)S(1)}, bf16[128,256]{1,0:T(8,128)(2,1)}, u32[]{:S(2)}) copy-start(bf16[128,256]{1,0:T(8,128)(2,1)} %param.13) | copy-start | bytes 196612
  8.4 56.5 %copy-start.1 = (bf16[4096,128]{1,0:T(8,128)(2,1)S(1)}, bf16[4096,128]{1,0:T(8,128)(2,1)}, u32[]{:S(2)}) copy-start(bf16[4096,128]{1,0:T(8,128)(2,1)} %own_ref.1) | copy-start | bytes 3145732
  8.4 56.5 %copy-start.3 = (bf16[128,256]{1,0:T(8,128)(2,1)S(1)}, bf16[128,256]{1,0:T(8,128)(2,1)}, u32[]{:S(2)}) copy-start(bf16[128,256]{1,0:T(8,128)(2,1)} %w_self.1) | copy-start | bytes 196612
  64.9 1.6 %copy-start.6 = (bf16[4096,256]{1,0:T(8,128)(2,1)S(1)}, bf16[4096,256]{1,0:T(8,128)(2,1)}, u32[]{:S(2)}) copy-start(bf16[4096,256]{1,0:T(8,128)(2,1)} %param.15) | copy-start | bytes 6291460
  64.9 1.6 %copy-start.7 = (f32[256]{0:T(256)S(1)}, f32[256]{0:T(256)}, u32[]{:S(2)}) copy-start(f32[256]{0:T(256)} %param.14) | copy-start | bytes 3076
  71.5 3.8 %copy-start.2 = (bf16[4096,256]{1,0:T(8,128)(2,1)}, bf16[4096,256]{1,0:T(8,128)(2,1)S(1)}, u32[]{:S(2)}) copy-start(bf16[4096,256]{1,0:T(8,128)(2,1)S(1)} %get-tuple-element.26.dz) | copy-start | bytes 6291460
  138.9 5.8 %copy-start.4 = (f32[8,32,256]{2,1,0:T(8,128)S(1)}, f32[8,32,256]{2,1,0:T(8,128)}, u32[]{:S(2)}) copy-start(f32[8,32,256]{2,1,0:T(8,128)} %get-tuple-element.23) | copy-start | bytes 786436
  138.9 6.5 %copy-start.5 = (f32[1,256]{1,0:T(1,128)S(1)}, f32[1,256]{1,0:T(1,128)}, u32[]{:S(2)}) copy-start(f32[1,256]{1,0:T(1,128)} %get-tuple-element.24) | copy-start | bytes 3076

commit v4 on v3

--- a/solution.py
+++ b/solution.py
@@ -10,88 +10,131 @@
 FANOUT = 10
 HALO = 1024
 UNROLL = 8
+GROUPS = (32, 4, 1)
+CHUNK = 256
 VMEM_LIMIT = 60 * 1024 * 1024
 
 
 def by_count(starts_ref, order_ref, visit):
     for live in range(1, FANOUT + 1):
         first, last = starts_ref[live - 1], starts_ref[live]
-        groups = lax.div(last - first, UNROLL)
-
-        def group(i, carry, first=first, live=live):
-            at = first + i * UNROLL
-            visit([order_ref[at + u] for u in range(UNROLL)], live)
-            return carry
-
-        def single(i, carry, live=live):
-            visit([order_ref[i]], live)
-            return carry
-
-        lax.fori_loop(0, groups, group, 0)
-        lax.fori_loop(first + groups * UNROLL, last, single, 0)
-
-
-def gather_kernel(
-    rows_ref, starts_ref, order_ref, lower_ref, own_ref, upper_ref, hub_ref, total_ref, table
+        for size in GROUPS:
+            groups = lax.div(last - first, size)
+
+            def group(i, carry, first=first, live=live, size=size):
+                at = first + i * size
+                visit([order_ref[at + u] for u in range(size)], live)
+                return carry
+
+            lax.fori_loop(0, groups, group, 0)
+            first = first + groups * size
+
+
+def layer_kernel(
+    rows_ref,
+    starts_ref,
+    order_ref,
+    lower_ref,
+    own_ref,
+    upper_ref,
+    hub_ref,
+    weights_ref,
+    bias_ref,
+    cotangent_ref,
+    act_out,
+    local_ref,
+    border_ref,
+    hub_grad_ref,
+    grads_ref,
+    table,
+    held,
+    cotangent,
+    act,
+    grad_w,
+    grad_b,
+    in_sem,
+    out_sem,
+    *sums,
 ):
+    kinds = len(sums)
+    extent, width = table.shape
+    nodes = own_ref.shape[0]
+    hidden = grad_w.shape[1]
+    load = pltpu.make_async_copy(cotangent_ref, cotangent, in_sem)
+    load.start()
     at = 0
     for part in (lower_ref, own_ref, upper_ref, hub_ref):
         size = part.shape[0]
         table[at : at + size, :] = part[...].astype(jnp.float32)
         at += size
 
-    def visit(nodes, live):
-        for n in nodes:
+    def gather(group, live):
+        for n in group:
             picked = [table[pl.ds(rows_ref[s, n], 1), :] for s in range(live)]
             while len(picked) > 1:
                 picked = [a + b for a, b in zip(picked[::2], picked[1::2])] + (
                     [picked[-1]] if len(picked) % 2 else []
                 )
-            total_ref[pl.ds(n, 1), :] = picked[0]
-
-    by_count(starts_ref, order_ref, visit)
-
-
-def gather_sum(rows, starts, order, lower, own, upper, hubs):
-    extent = lower.shape[0] + own.shape[0] + upper.shape[0] + hubs.shape[0]
-    vmem = pl.BlockSpec(memory_space=pltpu.VMEM)
-    return pl.pallas_call(
-        gather_kernel,
-        out_shape=jax.ShapeDtypeStruct(own.shape, jnp.float32),
-        in_specs=[pl.BlockSpec(memory_space=pltpu.SMEM)] * 3 + [vmem] * 4,
-        out_specs=vmem,
-        scratch_shapes=[pltpu.VMEM((extent, own.shape[1]), jnp.float32)],
-        compiler_params=pltpu.CompilerParams(vmem_limit_bytes=VMEM_LIMIT),
-        name="gather_sum",
-    )(rows, starts, order, lower, own, upper, hubs)
-
-
-def scatter_kernel(rows_ref, starts_ref, order_ref, source_ref, own_ref, border_ref, hub_ref, *sums):
-    chunk = 512
-    extent = sums[0].shape[0]
-    width = sums[0].shape[1]
-    kinds = len(sums)
+            held[pl.ds(n, 1), :] = picked[0] * (1.0 / live)
+
+    by_count(starts_ref, order_ref, gather)
+
+    load.wait()
+    grad_w[...] = jnp.zeros_like(grad_w)
+    grad_b[...] = jnp.zeros_like(grad_b)
+    slope, cubic = 0.7978845608028654, 0.044715
+
+    def dense(i, carry):
+        at = pl.ds(pl.multiple_of(i * CHUNK, CHUNK), CHUNK)
+        inputs = jnp.concatenate([own_ref[at, :], held[at, :].astype(jnp.bfloat16)], axis=1)
+        z = (
+            jnp.dot(inputs, weights_ref[...], preferred_element_type=jnp.float32) + bias_ref[...]
+        )
+        square = z * z
+        tilt = jnp.tanh(slope * (z + cubic * (square * z)))
+        half = 0.5 * (1.0 + tilt)
+        act[at, :] = (z * half).astype(jnp.bfloat16)
+        rise = half + 0.5 * z * ((1.0 - tilt * tilt) * (slope * (1.0 + 3.0 * cubic * square)))
+        dz = (cotangent[at, :].astype(jnp.float32) * rise).astype(jnp.bfloat16)
+        grad_w[...] += lax.dot_general(
+            inputs, dz, (((0,), (0,)), ((), ())), preferred_element_type=jnp.float32
+        )
+        grad_b[...] += jnp.sum(dz.astype(jnp.float32).reshape(CHUNK // 8, 8, hidden), axis=0)
+        back = lax.dot_general(
+            dz, weights_ref[...], (((1,), (1,)), ((), ())), preferred_element_type=jnp.float32
+        )
+        local_ref[at, :] = back[:, :width]
+        held[at, :] = back[:, width:]
+        return carry
+
+    lax.fori_loop(0, nodes // CHUNK, dense, 0)
+    store = pltpu.make_async_copy(act, act_out, out_sem)
+    store.start()
+    blocks, part = grads_ref.shape[0], grads_ref.shape[1] - 8
+    for k in range(blocks):
+        grads_ref[k, :part, :] = grad_w[k * part : (k + 1) * part, :]
+        grads_ref[k, part:, :] = grad_b[...]
 
     def clear(i, carry):
         for total in sums:
-            total[pl.ds(pl.multiple_of(i * chunk, chunk), chunk), :] = jnp.zeros(
-                (chunk, width), jnp.float32
+            total[pl.ds(pl.multiple_of(i * CHUNK, CHUNK), CHUNK), :] = jnp.zeros(
+                (CHUNK, width), jnp.float32
             )
         return carry
 
-    lax.fori_loop(0, extent // chunk, clear, 0)
-
-    def visit(nodes, live):
-        values = [source_ref[pl.ds(n, 1), :] for n in nodes]
-        edges = [(u, s) for u in range(len(nodes)) for s in range(live)]
+    lax.fori_loop(0, extent // CHUNK, clear, 0)
+
+    def scatter(group, live):
+        values = [held[pl.ds(n, 1), :] * (1.0 / live) for n in group]
+        edges = [(u, s) for u in range(len(group)) for s in range(live)]
         for first in range(0, len(edges), kinds):
             batch = edges[first : first + kinds]
-            rows = [rows_ref[s, nodes[u]] for u, s in batch]
-            held = [sums[k][pl.ds(row, 1), :] for k, row in enumerate(rows)]
+            rows = [rows_ref[s, group[u]] for u, s in batch]
+            old = [sums[k][pl.ds(row, 1), :] for k, row in enumerate(rows)]
             for k, (u, s) in enumerate(batch):
-                sums[k][pl.ds(rows[k], 1), :] = held[k] + values[u]
-
-    by_count(starts_ref, order_ref, visit)
+                sums[k][pl.ds(rows[k], 1), :] = old[k] + values[u]
+
+    by_count(starts_ref, order_ref, scatter)
 
     def added(at, size):
         total = sums[0][pl.ds(at, size), :]
@@ -99,39 +142,56 @@
             total = total + other[pl.ds(at, size), :]
         return total
 
-    def emit(ref, ref_at, at, count):
+    def emit(ref, ref_at, at, count, more):
         def one(i, carry):
             off = pl.multiple_of(i * 128, 128)
-            ref[pl.ds(ref_at + off, 128), :] = added(at + off, 128).astype(ref.dtype)
+            total = added(at + off, 128)
+            if more:
+                total = total + ref[pl.ds(ref_at + off, 128), :]
+            ref[pl.ds(ref_at + off, 128), :] = total.astype(ref.dtype)
             return carry
 
         lax.fori_loop(0, count // 128, one, 0)
 
-    nodes = own_ref.shape[0]
-    emit(border_ref, 0, 0, HALO)
-    emit(own_ref, 0, HALO, nodes)
-    emit(border_ref, HALO, HALO + nodes, HALO)
-    emit(hub_ref, 0, 2 * HALO + nodes, hub_ref.shape[0])
-
-
-def scatter_sum(rows, starts, order, source, hubs):
-    nodes, width = source.shape
-    extent = 2 * HALO + nodes + hubs
+    emit(border_ref, 0, 0, HALO, False)
+    emit(local_ref, 0, HALO, nodes, True)
+    emit(border_ref, HALO, HALO + nodes, HALO, False)
+    emit(hub_grad_ref, 0, 2 * HALO + nodes, hub_grad_ref.shape[0], False)
+    store.wait()
+
+
+def layer(rows, starts, order, lower, own, upper, hubs, weights, bias, cotangent, n_col):
+    nodes, width = own.shape
+    hidden = weights.shape[1]
+    extent = lower.shape[0] + nodes + upper.shape[0] + hubs.shape[0]
     kinds = 10 if extent <= 8192 else 5
     vmem = pl.BlockSpec(memory_space=pltpu.VMEM)
+    anywhere = pl.BlockSpec(memory_space=pl.ANY)
     return pl.pallas_call(
-        scatter_kernel,
+        layer_kernel,
         out_shape=(
+            jax.ShapeDtypeStruct((nodes, hidden), jnp.bfloat16),
             jax.ShapeDtypeStruct((nodes, width), jnp.float32),
             jax.ShapeDtypeStruct((2 * HALO, width), jnp.bfloat16),
-            jax.ShapeDtypeStruct((hubs, width), jnp.bfloat16),
+            jax.ShapeDtypeStruct(hubs.shape, jnp.bfloat16),
+            jax.ShapeDtypeStruct((n_col, 2 * width // n_col + 8, hidden), jnp.float32),
         ),
-        in_specs=[pl.BlockSpec(memory_space=pltpu.SMEM)] * 3 + [vmem],
-        out_specs=(vmem, vmem, vmem),
-        scratch_shapes=[pltpu.VMEM((extent, width), jnp.float32)] * kinds,
+        in_specs=[pl.BlockSpec(memory_space=pltpu.SMEM)] * 3 + [vmem] * 6 + [anywhere],
+        out_specs=(anywhere, vmem, vmem, vmem, vmem),
+        scratch_shapes=[
+            pltpu.VMEM((extent, width), jnp.float32),
+            pltpu.VMEM((nodes, width), jnp.float32),
+            pltpu.VMEM((nodes, hidden), jnp.bfloat16),
+            pltpu.VMEM((nodes, hidden), jnp.bfloat16),
+            pltpu.VMEM((2 * width, hidden), jnp.float32),
+            pltpu.VMEM((8, hidden), jnp.float32),
+            pltpu.SemaphoreType.DMA,
+            pltpu.SemaphoreType.DMA,
+        ]
+        + [pltpu.VMEM((extent, width), jnp.float32)] * kinds,
         compiler_params=pltpu.CompilerParams(vmem_limit_bytes=VMEM_LIMIT),
-        name="scatter_sum",
-    )(rows, starts, order, source)
+        name="layer",
+    )(rows, starts, order, lower, own, upper, hubs, weights, bias, cotangent)
 
 
 MESH = pl.DeviceIdType.MESH
@@ -433,18 +493,9 @@
     )(border, hub, grads)
 
 
-def finish_kernel(hub_rows, own, dz, w_self, rim, hub, out, total):
-    chunk = 512
+def finish_kernel(hub_rows, own, rim, hub, out, total):
     nodes = own.shape[0]
-
-    def back(i, carry):
-        at = pl.ds(pl.multiple_of(i * chunk, chunk), chunk)
-        total[at, :] = own[at, :] + lax.dot_general(
-            dz[at, :], w_self[...], (((1,), (1,)), ((), ())), preferred_element_type=jnp.float32
-        )
-        return carry
-
-    lax.fori_loop(0, nodes // chunk, back, 0)
+    total[...] = own[...]
     total[:HALO, :] += rim[:HALO, :].astype(jnp.float32)
     total[nodes - HALO :, :] += rim[HALO:, :].astype(jnp.float32)
 
@@ -459,57 +510,46 @@
     out[...] = total[...].astype(out.dtype)
 
 
-def finish(hub_rows, own, dz, w_self, rim, hub):
+def finish(hub_rows, own, rim, hub):
     vmem = pl.BlockSpec(memory_space=pltpu.VMEM)
     return pl.pallas_call(
         finish_kernel,
         out_shape=jax.ShapeDtypeStruct(own.shape, jnp.bfloat16),
-        in_specs=[pl.BlockSpec(memory_space=pltpu.SMEM)] + [vmem] * 5,
+        in_specs=[pl.BlockSpec(memory_space=pltpu.SMEM)] + [vmem] * 3,
         out_specs=vmem,
         scratch_shapes=[pltpu.VMEM(own.shape, jnp.float32)],
         compiler_params=pltpu.CompilerParams(vmem_limit_bytes=VMEM_LIMIT),
         name="finish",
-    )(hub_rows, own, dz, w_self, rim, hub)
-
-
-def gelu_tanh(value):
-    return jax.nn.gelu(value, approximate=True)
+    )(hub_rows, own, rim, hub)
 
 
 def on_device(features, neighbors, counts, hub_rows, w_self, w_neigh, out_bias, cotangent):
     node_count = features.shape[0]
     n_row, n_col = lax.axis_size("row"), lax.axis_size("col")
     lower, upper, hub_table = entry_exchange(features, hub_rows, n_row, n_col)
-    hubs = hub_table.shape[0]
     rows = neighbors.T
     keys = counts * node_count + jnp.arange(node_count, dtype=jnp.int32)
     order = lax.sort(keys, is_stable=False) % node_count
     starts = jnp.sum(
         counts[None, :] <= jnp.arange(FANOUT + 1)[:, None], axis=1, dtype=jnp.int32
     )
-    divisor = counts.astype(jnp.float32)[:, None]
-    agg = (gather_sum(rows, starts, order, lower, features, upper, hub_table) / divisor).astype(jnp.bfloat16)
-    pre = (
-        jnp.dot(features, w_self, preferred_element_type=jnp.float32)
-        + jnp.dot(agg, w_neigh, preferred_element_type=jnp.float32)
-        + out_bias
-    )
-    act, backward = jax.vjp(gelu_tanh, pre)
-    activations = act.astype(jnp.bfloat16)
-    dz = backward(cotangent.astype(jnp.float32))[0].astype(jnp.bfloat16)
-    dims = (((0,), (0,)), ((), ()))
-    back_dims = (((1,), (1,)), ((), ()))
-    grad_self = lax.dot_general(features, dz, dims, preferred_element_type=jnp.float32)
-    grad_b = jnp.sum(dz.astype(jnp.float32), axis=0)
-    grad_neigh = lax.dot_general(agg, dz, dims, preferred_element_type=jnp.float32)
-    source = lax.dot_general(dz, w_neigh, back_dims, preferred_element_type=jnp.float32) / divisor
-    mine, border, hub_grads = scatter_sum(rows, starts, order, source, hubs)
-    hidden = dz.shape[1]
-    blocks = jnp.concatenate([grad_self, grad_neigh], axis=0).reshape(n_col, -1, hidden)
-    grads = jnp.concatenate([blocks, jnp.broadcast_to(jnp.pad(grad_b[None, :], ((0, 7), (0, 0))), (n_col, 8, hidden))], axis=1)
+    stacked = jnp.concatenate([w_self, w_neigh], axis=0)
+    activations, mine, border, hub_grads, grads = layer(
+        rows,
+        starts,
+        order,
+        lower,
+        features,
+        upper,
+        hub_table,
+        stacked,
+        out_bias[None, :],
+        cotangent,
+        n_col,
+    )
     rim, hub_share, weights, bias = exit_exchange(border, hub_grads, grads, n_row, n_col)
-    grad_features = finish(hub_rows, mine, dz, w_self, rim, hub_share)
-    weights = weights.reshape(2, -1, hidden)
+    grad_features = finish(hub_rows, mine, rim, hub_share)
+    weights = weights.reshape(2, -1, weights.shape[2])
     grad_self, grad_neigh, grad_b = weights[0], weights[1], bias[0]
     return (activations, grad_features, grad_self, grad_neigh, grad_b)
 

time: 147 us -> 135 us (0.918)
  matrix products: 8.61 us -> 0 us
    dot_general x5 -> x0, matrix products: 8.61 us -> none  [the longest x1 4.96 us: on_device(): jnp.dot(agg, w_neigh, preferred_element_type=jnp.float32)]
    convert_element_type x2 -> x0, other arithmetic: 2.74 us -> none  [the longest x1 1.94 us: on_device(): (gather_sum(rows, starts, order, lower, features, upper, hub_table) / div...]
    pallas_call x1, Pallas kernels: 5.76 us -> 3.45 us  [finish(): pl.pallas_call(finish_kernel, out_shape=jax.ShapeDtypeStruct(own.shape, j...]
    pallas_call x2 -> x1, Pallas kernels: 84.9 us -> 85.4 us  [layer(): pl.pallas_call(layer_kernel, out_shape=(jax.ShapeDtypeStruct((nodes, hidd...]
where the time goes in v4:
time: 135 us
  Pallas kernels  123 us (91%)
  other arithmetic  9.19 us (7%)
    pallas_call x1, Pallas kernels, layer(): pl.pallas_call(layer_kernel, out_shape=(jax.ShapeDtypeStruct((nodes, hidd...  85.4 us
    pallas_call x1, Pallas kernels, exit_exchange(): pl.pallas_call(functools.partial(exit_kernel, n_row, n_col), out_shape=(j...  20.9 us
    pallas_call x1, Pallas kernels, entry_exchange(): pl.pallas_call(functools.partial(entry_kernel, n_row, n_col), out_shape=(...  13.6 us
    sort x1, other arithmetic, on_device(): order = lax.sort(keys, is_stable=False) % node_count  4.92 us
    pallas_call x1, Pallas kernels, finish(): pl.pallas_call(finish_kernel, out_shape=jax.ShapeDtypeStruct(own.shape, j...  3.45 us

profile of v4, /device:TPU:0, one launch (start us, length us, event | category | flops | bytes accessed | tf_op | source)
XLA Modules:
  0.0 134.6 jit_solution(4028222138436514759)
XLA Ops:
  0.6 1.4 %convert_reduce_fusion.starts_ref = s32[11]{0:T(128)} fusion(s32[4096]{0:T(1024)} %param.10), kind=kLoop, calls=%fused_computation | loop fusion | flops 135157 | bytes 16428 | tf_op jit(solution)/shard_map/reduce_sum | solution.py:533
  2.0 0.7 iota_add_fusion
  2.7 4.9 %sort.7 = s32[4096]{0:T(1024)S(1)} sort(s32[4096]{0:T(1024)S(1)} %iota_add_fusion), dimensions={0}, to_apply=%region_1.2 | sort | flops 49152 | bytes 32768 | tf_op jit(solution)/shard_map/sort | solution.py:532
  7.6 0.6 add_select_fusion.order_ref
  8.3 1.5 %pad_maximum_fusion.weights_ref = bf16[256,256]{1,0:T(8,128)(2,1)} fusion(bf16[128,256]{1,0:T(8,128)(2,1)} %param.13, bf16[128,256]{1,0:T(8,128)(2,1)} %param.12), kind=kLoop, calls=%fused_computation.2 | loop fusion | flops 262144 | bytes 262144 | tf_op jit(solution)/shard_map/concatenate | solution.py:536
  9.8 13.6 %entry_exchange.1 = (bf16[1024,128]{1,0:T(8,128)(2,1)}, bf16[1024,128]{1,0:T(8,128)(2,1)}, bf16[1024,128]{1,0:T(8,128)(2,1)}) custom-call(s32[128]{0:T(128)} %hub_rows.3, bf16[4096,128]{1,0:T(8,128)(2,1)} %own_ref.1), custom_call_target="tpu_custom_call" | custom-call | tf_op jit(solution)/shard_map/entry_exchange/pallas_call | solution.py:316
  23.5 85.4 %layer.1 = (bf16[4096,256]{1,0:T(8,128)(2,1)}, f32[4096,128]{1,0:T(8,128)}, bf16[2048,128]{1,0:T(8,128)(2,1)}, bf16[1024,128]{1,0:T(8,128)(2,1)}, f32[8,40,256]{2,1,0:T(8,128)}) custom-call(s32[10,4096]{1,0:T(8,128)} %bitcast.5, s32[11]{0:T(128)} %convert_reduce_fusion.starts_ref, s32[4096]{0:T(1024)} %add_select_fusion.order_ref, ...), custom_call_target="tpu_custom_call" | custom-call | tf_op jit(solution)/shard_map/layer/pallas_call | solution.py:170
  108.9 20.9 %exit_exchange.1 = (bf16[2048,128]{1,0:T(8,128)(2,1)}, f32[128,128]{1,0:T(8,128)}, f32[8,32,256]{2,1,0:T(8,128)}, f32[1,256]{1,0:T(1,128)}) custom-call(bf16[2048,128]{1,0:T(8,128)(2,1)} %get-tuple-element.22.border, bf16[1024,128]{1,0:T(8,128)(2,1)} %get-tuple-element.23.hub, f32[8,40,256]{2,1,0:T(8,128)} %get-tuple-element.24.grads), custom_call_target="tpu_custom_call" | custom-call | tf_op jit(solution)/shard_map/exit_exchange/pallas_call | solution.py:469
  129.8 0.0 copy-start
  129.8 0.0 copy-start.1
  129.8 3.4 %finish.1 = bf16[4096,128]{1,0:T(8,128)(2,1)} custom-call(s32[128]{0:T(128)} %hub_rows.3, f32[4096,128]{1,0:T(8,128)} %get-tuple-element.21.own, bf16[2048,128]{1,0:T(8,128)(2,1)} %get-tuple-element.25.rim, f32[128,128]{1,0:T(8,128)} %get-tuple-element.26.hub), custom_call_target="tpu_custom_call" | custom-call | tf_op jit(solution)/shard_map/finish/pallas_call | solution.py:515
  133.3 0.0 copy-done
  133.3 0.7 fusion.1
  134.0 0.0 copy-done.1
  134.0 0.6 copy.14
Async XLA Ops:
  129.8 3.5 %copy-start = (f32[8,32,256]{2,1,0:T(8,128)S(1)}, f32[8,32,256]{2,1,0:T(8,128)}, u32[]{:S(2)}) copy-start(f32[8,32,256]{2,1,0:T(8,128)} %get-tuple-element.27) | copy-start | bytes 786436
  129.8 4.2 %copy-start.1 = (f32[1,256]{1,0:T(1,128)S(1)}, f32[1,256]{1,0:T(1,128)}, u32[]{:S(2)}) copy-start(f32[1,256]{1,0:T(1,128)} %get-tuple-element.28) | copy-start | bytes 3076
